TPU v7x, 256 devices: a whole 4x4x8 slice. The times are simulated.
256 devices in a mesh: gx: 16 (over z_hi, x), gy: 16 (over z_lo, y, core).
Axes of the slice: x: 4, y: 4, z: 8 (z_hi: 4, z_lo: 2; z = z_hi * 2 + z_lo), core: 2. Of those that a mesh axis runs over, the one named last changes fastest.
Arguments:
- positions: float32 [3, 32, 32, 128], P(None, 'gx', 'gy'), may hold values from 0 to 192, as said below
- valid_mask: int32 [32, 32, 128], P('gx', 'gy'), may hold values from 0 to 1, as said below
- species: int32 [32, 32, 128], P('gx', 'gy'), may hold values from 0 to 3
- density_table: float32 [32, 256], replicated, may hold values from -1 to 1
- radial_gain: float32 [8, 256], replicated, may hold values from -4 to 4
- readout: bfloat16 [256, 16], replicated, may hold values from -0.375 to 0.375
Outputs:
- forces: float32 [3, 32, 32, 128], P(None, 'gx', 'gy')
- energies: float32 [16, 32, 32, 128], P(None, 'gx', 'gy')
Inputs may be any that keep to these rules, and one draw needn't show every extreme that they name: `positions`: the atoms of cell (a, b) lie at x in [6 a, 6 a + 6), y in [6 b, 6 b + 6) and z in [0, 0.3 * 128). `valid_mask`: in each cell the slots holding 1 come before those holding 0.
All inputs are finite; a program needn't handle non-finite values.
Results may differ from a plain program's by a relative error of at most 0.0095.
Values sent between devices are 32-bit elements; how exact they have to be, the bound alone decides.
A program may use at most 128 MiB of HBM per device.

v0:
```python
import jax
import jax.numpy as jnp
from jax import lax
from jax.sharding import PartitionSpec as P

RADIAL = 8
SPECIES = 4


cutoff_radius = 6.0
soften_sq = 0.01
norm_one = 8.0
norm_two = 32.0


def extended(x, sides, width):
    for axis, dim in sides:
        peers, length = (lax.axis_size(axis), x.shape[dim])
        up = [(i, (i + 1) % peers) for i in range(peers - 1)]
        down = [(j, i) for i, j in up]
        last = lax.slice_in_dim(x, length - width, length, axis=dim)
        first = lax.slice_in_dim(x, 0, width, axis=dim)
        before = lax.ppermute(last, axis, up)
        after = lax.ppermute(first, axis, down)
        x = jnp.concatenate([before, x, after], axis=dim)
    return x


def pair_basis(near_pos, near_valid):
    count = near_pos.shape[-1]
    own_pos = near_pos[:, 1, 1, :]
    own_valid = near_valid[1, 1, :]
    flat_pos = near_pos.reshape(3, 9, count)
    flat_valid = near_valid.reshape(9, count)
    offset = own_pos[:, :, None, None] - flat_pos[:, None, :, :]
    distance = jnp.sqrt(jnp.sum(offset * offset, axis=0) + soften_sq)
    reach = jnp.maximum(1.0 - jnp.square(distance / cutoff_radius), 0.0)
    atom_ids = jnp.arange(count, dtype=jnp.int32)
    cell_ids = jnp.arange(9, dtype=jnp.int32)
    self_pair = (atom_ids[:, None, None] == atom_ids[None, None, :]) & (
        cell_ids[None, :, None] == 4
    )
    weight = (
        own_valid[:, None, None]
        * flat_valid[None, :, :]
        * jnp.where(self_pair, 0.0, 1.0)
        * reach
        * reach
    )
    spacing = cutoff_radius / (RADIAL - 1)
    centres = jnp.arange(RADIAL, dtype=jnp.float32) * spacing
    gaussian = jnp.exp(
        -jnp.square((distance[:, :, None, :] - centres[None, None, :, None]) / spacing)
    )
    return weight[:, :, None, :] * gaussian


def density_block(near_pos, near_valid, near_species):
    count = near_pos.shape[-1]
    radial_basis = pair_basis(near_pos, near_valid)
    kinds = jnp.arange(SPECIES, dtype=jnp.float32)
    onehot = (near_species.reshape(9, count)[:, :, None] == kinds[None, None, :]).astype(
        jnp.float32
    )
    density = jnp.einsum("icku,cus->iks", radial_basis, onehot, precision=lax.Precision.HIGHEST)
    return density.reshape(count, RADIAL * SPECIES)


def cell_densities(pos_padded, valid_padded, species_padded):
    span_x = pos_padded.shape[1] - 2
    span_y = pos_padded.shape[2] - 2
    count = pos_padded.shape[3]

    def cell_one_cell(cell_index):
        zero = jnp.zeros((), jnp.int32)
        row_index = cell_index // span_y
        col_index = cell_index % span_y
        near_pos = lax.dynamic_slice(
            pos_padded, (zero, row_index, col_index, zero), (3, 3, 3, count)
        )
        near_valid = lax.dynamic_slice(valid_padded, (row_index, col_index, zero), (3, 3, count))
        near_species = lax.dynamic_slice(
            species_padded, (row_index, col_index, zero), (3, 3, count)
        )
        return density_block(near_pos, near_valid, near_species)

    density = lax.map(jax.checkpoint(cell_one_cell), jnp.arange(span_x * span_y, dtype=jnp.int32))
    return density.reshape(span_x, span_y, count, RADIAL * SPECIES)


def activate(density, density_table):
    product = jnp.dot(
        density, density_table, precision=lax.Precision.HIGHEST, preferred_element_type=jnp.float32
    )
    return jax.nn.silu(product / norm_one)


def cell_energy(near_pos, near_hidden, near_valid, radial_gain, readout):
    count = near_pos.shape[-1]
    width = near_hidden.shape[-1]
    radial_basis = (
        pair_basis(near_pos, near_valid).astype(jnp.bfloat16).reshape(count, 9 * RADIAL * count)
    )
    scaled = (near_hidden.reshape(9, 1, count, width) * radial_gain[None, :, None, :]).astype(
        jnp.bfloat16
    )
    scaled = scaled.reshape(9 * RADIAL * count, width)
    message = jnp.dot(radial_basis, scaled, preferred_element_type=jnp.float32)
    hidden_two = jax.nn.silu(message / norm_two + near_hidden[1, 1]).astype(jnp.bfloat16)
    head_input = jnp.dot(hidden_two, readout, preferred_element_type=jnp.float32)
    return (near_valid[1, 1][:, None] * jax.nn.silu(head_input)).T


def layer_two(pos_padded, hidden_padded, valid_padded, radial_gain, readout):
    span_x = pos_padded.shape[1] - 2
    span_y = pos_padded.shape[2] - 2
    count = pos_padded.shape[3]
    width = hidden_padded.shape[3]

    def layer_one_cell(cell_index):
        zero = jnp.zeros((), jnp.int32)
        row_index = cell_index // span_y
        col_index = cell_index % span_y
        near_pos = lax.dynamic_slice(
            pos_padded, (zero, row_index, col_index, zero), (3, 3, 3, count)
        )
        near_hidden = lax.dynamic_slice(
            hidden_padded, (row_index, col_index, zero, zero), (3, 3, count, width)
        )
        near_valid = lax.dynamic_slice(valid_padded, (row_index, col_index, zero), (3, 3, count))
        return cell_energy(near_pos, near_hidden, near_valid, radial_gain, readout)

    return lax.map(jax.checkpoint(layer_one_cell), jnp.arange(span_x * span_y, dtype=jnp.int32))


def take_range(array, dim, low, high):
    return lax.slice_in_dim(array, low, high, axis=dim)


def place_edges(first, last, dim, length):
    shape = list(first.shape)
    shape[dim] = length - 2
    return jnp.concatenate([first, jnp.zeros(shape, first.dtype), last], axis=dim)


def edge_slot(array, dim_x, slot_kind):
    dim_y = dim_x + 1
    size_x = array.shape[dim_x]
    size_y = array.shape[dim_y]
    if slot_kind == 0:
        inner = take_range(array, dim_y, 1, size_y - 1)
        return place_edges(
            take_range(inner, dim_x, 0, 1),
            take_range(inner, dim_x, size_x - 1, size_x),
            dim_x,
            size_x - 2,
        )
    if slot_kind == 1:
        inner = take_range(array, dim_x, 1, size_x - 1)
        return place_edges(
            take_range(inner, dim_y, 0, 1),
            take_range(inner, dim_y, size_y - 1, size_y),
            dim_y,
            size_y - 2,
        )
    low_side = take_range(array, dim_x, 0, 1)
    high_side = take_range(array, dim_x, size_x - 1, size_x)
    row_low = place_edges(
        take_range(low_side, dim_y, 0, 1),
        take_range(low_side, dim_y, size_y - 1, size_y),
        dim_y,
        size_y - 2,
    )
    row_high = place_edges(
        take_range(high_side, dim_y, 0, 1),
        take_range(high_side, dim_y, size_y - 1, size_y),
        dim_y,
        size_y - 2,
    )
    return place_edges(row_low, row_high, dim_x, size_x - 2)


def slot_stack(array, dim_x):
    return jnp.stack(
        [edge_slot(array, dim_x, 0), edge_slot(array, dim_x, 1), edge_slot(array, dim_x, 2)], 0
    )


def slot_merge(array, received, dim_x):
    interior = take_range(array, dim_x, 1, array.shape[dim_x] - 1)
    interior = take_range(interior, dim_x + 1, 1, array.shape[dim_x + 1] - 1)
    return (
        interior
        + edge_slot(received[0], dim_x, 0)
        + edge_slot(received[1], dim_x, 1)
        + edge_slot(received[2], dim_x, 2)
    )


def return_features(grad_padded):
    received = extended(slot_stack(grad_padded, 0), (("gx", 1), ("gy", 2)), 1)
    return slot_merge(grad_padded, received, 0)


def return_forces(grad_padded):
    received = extended(slot_stack(grad_padded, 1), (("gx", 2), ("gy", 3)), 1)
    return slot_merge(grad_padded, received, 1)


def shards(positions, valid_mask, species, density_table, radial_gain, readout):
    atoms = jnp.concatenate(
        [positions, valid_mask.astype(jnp.float32)[None], species.astype(jnp.float32)[None]], 0
    )
    padded_atoms = extended(atoms, (("gx", 1), ("gy", 2)), 1)
    pos_padded = padded_atoms[:3]
    valid_padded = padded_atoms[3]
    species_padded = padded_atoms[4]

    def densities_of(coords):
        return cell_densities(coords, valid_padded, species_padded)

    def activate_with(density):
        return activate(density, density_table)

    def energy_of(coords, hidden_padded):
        return layer_two(coords, hidden_padded, valid_padded, radial_gain, readout)

    density, density_back = jax.vjp(densities_of, pos_padded)
    hidden, activate_back = jax.vjp(activate_with, density)
    hidden_padded = extended(hidden, (("gx", 0), ("gy", 1)), 1)
    energy, energy_back = jax.vjp(energy_of, pos_padded, hidden_padded)
    heads_count = energy.shape[1]
    pos_grad_two, hidden_grad = energy_back(jnp.full(energy.shape, 1.0 / heads_count, jnp.float32))
    early_grad = return_forces(pos_grad_two)
    hidden_local = return_features(hidden_grad)
    (density_grad,) = activate_back(hidden_local)
    (pos_grad_one,) = density_back(density_grad)
    gradient = early_grad + return_forces(pos_grad_one)
    span_x = positions.shape[1]
    span_y = positions.shape[2]
    energies = energy.reshape(span_x, span_y, heads_count, energy.shape[2]).transpose(2, 0, 1, 3)
    return (-gradient, energies)


def solution(mesh):
    in_specs = (P(None, "gx", "gy", None), P("gx", "gy", None), P("gx", "gy", None), P(), P(), P())
    out_specs = (P(None, "gx", "gy", None), P(None, "gx", "gy", None))
    return jax.shard_map(shards, mesh=mesh, in_specs=in_specs, out_specs=out_specs, check_vma=False)
```

profile of v0, /device:TPU:95, one launch (start us, length us, event | category | flops | bytes accessed | tf_op | source)
XLA Modules:
  0.0 430.7 jit_solution(683078832382273459)
XLA Ops:
  2.7 6.0 %collective-permute-start = (f32[5,1,2,128]{3,0,2,1:T(8,128)S(1)}, f32[5,1,2,128]{3,0,2,1:T(8,128)S(1)}, u32[]{:S(2)}, u32[]{:S(2)}) collective-permute-start(f32[5,1,2,128]{3,0,2,1:T(8,128)S(1)} %get-tuple-element.982), channel_id=1, source_target_pairs={{0,16},{16,32},{32,48},{48,64},{64,80},{80,96},{96,112},{112,128},... | collective-permute-start | bytes 15368 | tf_op jit(solution)/shard_map/ppermute | solution.py:23
  10.7 6.7 %collective-permute-done.1 = f32[5,1,2,128]{3,0,2,1:T(8,128)S(1)} collective-permute-done((f32[5,1,2,128]{3,0,2,1:T(8,128)S(1)}, f32[5,1,2,128]{3,0,2,1:T(8,128)S(1)}, u32[]{:S(2)}, u32[]{:S(2)}) %collective-permute-start.1) | collective-permute-done | bytes 5152 | tf_op jit(solution)/shard_map/ppermute | solution.py:24
  17.4 4.3 collective-permute-start.2
  23.7 5.2 %collective-permute-done.3 = f32[5,4,1,128]{3,0,2,1:T(8,128)S(1)} collective-permute-done((f32[5,4,1,128]{3,0,2,1:T(8,128)S(1)}, f32[5,4,1,128]{3,0,2,1:T(8,128)S(1)}, u32[]{:S(2)}, u32[]{:S(2)}) %collective-permute-start.3) | collective-permute-done | bytes 10272 | tf_op jit(solution)/shard_map/ppermute | solution.py:24
  29.0 28.6 %while.62 = (s32[]{:T(128)}, f32[4,128,32]{1,2,0:T(8,128)S(1)}, s32[4]{0:T(128)S(1)}, f32[4,4,128]{2,1,0:T(4,128)S(1)}, f32[3,4,4,128]{3,0,2,1:T(4,128)S(1)}, /*...) while((s32[]{:T(128)}, f32[4,128,32]{1,2,0:T(8,128)S(1)}, ...), condition=%wide.region_2.3_spmd.clone, body=%wide.region_0.2_spmd.clone.sunk | while | flops 65327652 | bytes 3726357 | solution.py:87
  32.9 3.2 fusion.253
  40.1 3.2 fusion.253
  47.3 3.2 fusion.253
  54.4 3.2 fusion.253
  61.1 3.4 collective-permute-start.5
  64.4 3.9 collective-permute-done.4
  68.3 7.1 %collective-permute-done.5 = f32[1,2,128,256]{3,2,1,0:T(8,128)S(1)} collective-permute-done((f32[1,2,128,256]{3,2,1,0:T(8,128)S(1)}, f32[1,2,128,256]{3,2,1,0:T(8,128)S(1)}, u32[]{:S(2)}, u32[]{:S(2)}) %collective-permute-start.5) | collective-permute-done | bytes 262176 | tf_op jit(solution)/shard_map/ppermute | solution.py:24
  75.6 5.1 %collective-permute-start.6 = (f32[4,1,128,256]{3,2,1,0:T(8,128)S(1)}, f32[4,1,128,256]{3,2,1,0:T(8,128)S(1)}, u32[]{:S(2)}, u32[]{:S(2)}) collective-permute-start(f32[4,1,128,256]{3,2,1,0:T(8,128)S(1)} %get-tuple-element.924), channel_id=1, source_target_pairs={{0,1},{1,2},{2,3},{3,4},{4,5},{5,6},{6,7},{7,8},{8,9},{9,10},{10,1... | collective-permute-start | bytes 1572872 | tf_op jit(solution)/shard_map/ppermute | solution.py:23
  82.8 4.0 collective-permute-done.6
  86.8 6.5 %collective-permute-done.7 = f32[4,1,128,256]{3,2,1,0:T(8,128)S(1)} collective-permute-done((f32[4,1,128,256]{3,2,1,0:T(8,128)S(1)}, f32[4,1,128,256]{3,2,1,0:T(8,128)S(1)}, u32[]{:S(2)}, u32[]{:S(2)}) %collective-permute-start.7) | collective-permute-done | bytes 524320 | tf_op jit(solution)/shard_map/ppermute | solution.py:24
  96.5 153.3 %while.60 = (s32[]{:T(128)}, f32[3,4,4,128]{3,2,1,0:T(4,128)S(1)}, f32[4,4,128,256]{3,2,1,0:T(8,128)}, s32[4]{0:T(128)S(1)}, f32[3,4,4,128]{3,0,2,1:T(4,128)S(1)...) while((s32[]{:T(128)}, f32[3,4,4,128]{3,2,1,0:T(4,128)S(1)}, ...), condition=%wide.region_10.11_spmd, body=%wide.region_3.10_spmd.sunk | while | flops 1874307456 | bytes 72766664 | solution.py:133
  102.3 3.3 fusion.238
  113.3 3.8 fusion.241
  117.0 6.0 %copy.143 = f32[128,9216]{0,1:T(8,128)} copy(f32[128,9216]{1,0:T(8,128)} %fusion.241) | data formatting | bytes 9437184 | tf_op jit(solution)/shard_map/transpose(jvp())/while/body/eval_jaxpr/checkpoint/convert_element_type | solution.py:102
  123.1 5.2 %fusion.242 = (f32[128,9,128]{0,2,1:T(8,128)}, f32[128,9,128]{0,2,1:T(8,128)}) fusion(f32[128,9,8,128]{0,3,2,1:T(8,128)} %bitcast.304, f32[8]{0:T(128)S(1)} %iota_multiply_fusion.4, f32[128,9,128]{0,2,1:T(8,128)S(1)} %copy.141, f32[128,9,128]{0,2,1:T(8,128)S(1)} %copy.142), kind=kLoop, calls=%fused_computation.24.clone.1 | loop fusion | flops 15040512 | bytes 7077920 | tf_op jit(solution)/shard_map/transpose(jvp())/while/body/eval_jaxpr/checkpoint/reduce_sum | solution.py:55
  140.6 3.3 fusion.238
  151.6 3.8 fusion.241
  155.4 6.0 %copy.143 = f32[128,9216]{0,1:T(8,128)} copy(f32[128,9216]{1,0:T(8,128)} %fusion.241) | data formatting | bytes 9437184 | tf_op jit(solution)/shard_map/transpose(jvp())/while/body/eval_jaxpr/checkpoint/convert_element_type | solution.py:102
  161.4 5.2 %fusion.242 = (f32[128,9,128]{0,2,1:T(8,128)}, f32[128,9,128]{0,2,1:T(8,128)}) fusion(f32[128,9,8,128]{0,3,2,1:T(8,128)} %bitcast.304, f32[8]{0:T(128)S(1)} %iota_multiply_fusion.4, f32[128,9,128]{0,2,1:T(8,128)S(1)} %copy.141, f32[128,9,128]{0,2,1:T(8,128)S(1)} %copy.142), kind=kLoop, calls=%fused_computation.24.clone.1 | loop fusion | flops 15040512 | bytes 7077920 | tf_op jit(solution)/shard_map/transpose(jvp())/while/body/eval_jaxpr/checkpoint/reduce_sum | solution.py:55
  179.0 3.3 fusion.238
  189.9 3.8 fusion.241
  193.7 6.0 %copy.143 = f32[128,9216]{0,1:T(8,128)} copy(f32[128,9216]{1,0:T(8,128)} %fusion.241) | data formatting | bytes 9437184 | tf_op jit(solution)/shard_map/transpose(jvp())/while/body/eval_jaxpr/checkpoint/convert_element_type | solution.py:102
  199.7 5.2 %fusion.242 = (f32[128,9,128]{0,2,1:T(8,128)}, f32[128,9,128]{0,2,1:T(8,128)}) fusion(f32[128,9,8,128]{0,3,2,1:T(8,128)} %bitcast.304, f32[8]{0:T(128)S(1)} %iota_multiply_fusion.4, f32[128,9,128]{0,2,1:T(8,128)S(1)} %copy.141, f32[128,9,128]{0,2,1:T(8,128)S(1)} %copy.142), kind=kLoop, calls=%fused_computation.24.clone.1 | loop fusion | flops 15040512 | bytes 7077920 | tf_op jit(solution)/shard_map/transpose(jvp())/while/body/eval_jaxpr/checkpoint/reduce_sum | solution.py:55
  217.3 3.3 fusion.238
  228.2 3.8 fusion.241
  232.0 6.0 %copy.143 = f32[128,9216]{0,1:T(8,128)} copy(f32[128,9216]{1,0:T(8,128)} %fusion.241) | data formatting | bytes 9437184 | tf_op jit(solution)/shard_map/transpose(jvp())/while/body/eval_jaxpr/checkpoint/convert_element_type | solution.py:102
  238.1 5.2 %fusion.242 = (f32[128,9,128]{0,2,1:T(8,128)}, f32[128,9,128]{0,2,1:T(8,128)}) fusion(f32[128,9,8,128]{0,3,2,1:T(8,128)} %bitcast.304, f32[8]{0:T(128)S(1)} %iota_multiply_fusion.4, f32[128,9,128]{0,2,1:T(8,128)S(1)} %copy.141, f32[128,9,128]{0,2,1:T(8,128)S(1)} %copy.142), kind=kLoop, calls=%fused_computation.24.clone.1 | loop fusion | flops 15040512 | bytes 7077920 | tf_op jit(solution)/shard_map/transpose(jvp())/while/body/eval_jaxpr/checkpoint/reduce_sum | solution.py:55
  256.7 3.4 collective-permute-start.13
  260.2 6.1 %collective-permute-start.8 = (f32[3,3,1,2,128]{4,3,2,1,0:T(2,128)S(1)}, f32[3,3,1,2,128]{4,3,2,1,0:T(2,128)S(1)}, u32[]{:S(2)}, u32[]{:S(2)}) collective-permute-start(f32[3,3,1,2,128]{4,3,2,1,0:T(2,128)S(1)} %get-tuple-element.978), channel_id=1, source_target_pairs={{0,16},{16,32},{32,48},{48,64},{64,80},{80,96},{96,112},{112,128},... | collective-permute-start | bytes 27656 | tf_op jit(solution)/shard_map/ppermute | solution.py:23
  268.3 9.5 %collective-permute-done.8 = f32[3,3,1,2,128]{4,3,2,1,0:T(2,128)S(1)} collective-permute-done((f32[3,3,1,2,128]{4,3,2,1,0:T(2,128)S(1)}, f32[3,3,1,2,128]{4,3,2,1,0:T(2,128)S(1)}, u32[]{:S(2)}, u32[]{:S(2)}) %collective-permute-start.8) | collective-permute-done | bytes 9248 | tf_op jit(solution)/shard_map/ppermute | solution.py:23
  277.8 6.6 %collective-permute-done.9 = f32[3,3,1,2,128]{4,3,2,1,0:T(2,128)S(1)} collective-permute-done((f32[3,3,1,2,128]{4,3,2,1,0:T(2,128)S(1)}, f32[3,3,1,2,128]{4,3,2,1,0:T(2,128)S(1)}, u32[]{:S(2)}, u32[]{:S(2)}) %collective-permute-start.9) | collective-permute-done | bytes 9248 | tf_op jit(solution)/shard_map/ppermute | solution.py:24
  284.5 12.8 %collective-permute-start.10 = (f32[3,3,4,1,128]{4,3,2,1,0:T(1,128)S(1)}, f32[3,3,4,1,128]{4,3,2,1,0:T(1,128)S(1)}, u32[]{:S(2)}, u32[]{:S(2)}) collective-permute-start(f32[3,3,4,1,128]{4,3,2,1,0:T(1,128)S(1)} %get-tuple-element.940), channel_id=1, source_target_pairs={{0,1},{1,2},{2,3},{3,4},{4,5},{5,6},{6,7},{7,8},{8,9},{9,10},{10,1... | collective-permute-start | bytes 55304 | tf_op jit(solution)/shard_map/ppermute | solution.py:23
  302.4 5.7 %collective-permute-start.14 = (f32[3,4,1,128,256]{4,3,2,1,0:T(8,128)}, f32[3,4,1,128,256]{4,3,2,1,0:T(8,128)}, u32[]{:S(2)}, u32[]{:S(2)}) collective-permute-start(f32[3,4,1,128,256]{4,3,2,1,0:T(8,128)} %get-tuple-element.908), channel_id=1, source_target_pairs={{0,1},{1,2},{2,3},{3,4},{4,5},{5,6},{6,7},{7,8},{8,9},{9,10},{10,1... | collective-permute-start | bytes 4718600 | tf_op jit(solution)/shard_map/ppermute | solution.py:23
  310.7 43.7 %while.63 = (s32[]{:T(128)}, f32[4,16,128]{2,0,1:T(4,128)}, s32[4]{0:T(128)}, f32[4,4,128]{2,1,0:T(4,128)S(1)}, f32[3,4,4,128]{3,0,2,1:T(4,128)S(1)}, /*index=5*...) while((s32[]{:T(128)}, f32[4,16,128]{2,0,1:T(4,128)}, ...), condition=%wide.region_20.21_spmd.clone, body=%wide.region_18.20_spmd.clone.sunk | while | flops 619866176 | bytes 7365685 | solution.py:133
  363.0 42.1 %while.61 = (s32[]{:T(128)}, f32[3,4,4,128]{3,2,1,0:T(4,128)S(1)}, s32[4]{0:T(128)S(1)}, f32[4,128,32]{1,2,0:T(8,128)S(1)}, f32[3,4,4,128]{3,0,2,1:T(4,128)S(1)}...) while((s32[]{:T(128)}, f32[3,4,4,128]{3,2,1,0:T(4,128)S(1)}, ...), condition=%wide.region_17.18_spmd, body=%wide.region_11.17_spmd.sunk | while | flops 80538544 | bytes 8105023 | solution.py:87
  367.0 5.1 %fusion.248 = (f32[128,9,128]{2,0,1:T(8,128)S(1)}, f32[128,9,128]{2,0,1:T(8,128)S(1)}) fusion(f32[8]{0:T(128)S(1)} %iota_multiply_fusion.5, f32[128,9,128]{2,0,1:T(8,128)S(1)} %get-tuple-element.1234, f32[128,9,128]{2,0,1:T(8,128)S(1)} %get-tuple-element.1235, f32[128,8,4,1]{0,2,3,1:T(4,128)S(1)} %bitcast.319, f32[9,128]{1,0:T(8,128)S(1)} %eq.309), kind=kOutput, calls=%fused_computation.107.clone.1 | convolution fusion | flops 71668224 | bytes 2380320 | tf_op jit(solution)/shard_map/transpose(jvp())/while/body/eval_jaxpr/checkpoint/icku,cus->iks/dot_general | solution.py:65
  377.5 5.1 %fusion.248 = (f32[128,9,128]{2,0,1:T(8,128)S(1)}, f32[128,9,128]{2,0,1:T(8,128)S(1)}) fusion(f32[8]{0:T(128)S(1)} %iota_multiply_fusion.5, f32[128,9,128]{2,0,1:T(8,128)S(1)} %get-tuple-element.1234, f32[128,9,128]{2,0,1:T(8,128)S(1)} %get-tuple-element.1235, f32[128,8,4,1]{0,2,3,1:T(4,128)S(1)} %bitcast.319, f32[9,128]{1,0:T(8,128)S(1)} %eq.309), kind=kOutput, calls=%fused_computation.107.clone.1 | convolution fusion | flops 71668224 | bytes 2380320 | tf_op jit(solution)/shard_map/transpose(jvp())/while/body/eval_jaxpr/checkpoint/icku,cus->iks/dot_general | solution.py:65
  388.0 5.1 %fusion.248 = (f32[128,9,128]{2,0,1:T(8,128)S(1)}, f32[128,9,128]{2,0,1:T(8,128)S(1)}) fusion(f32[8]{0:T(128)S(1)} %iota_multiply_fusion.5, f32[128,9,128]{2,0,1:T(8,128)S(1)} %get-tuple-element.1234, f32[128,9,128]{2,0,1:T(8,128)S(1)} %get-tuple-element.1235, f32[128,8,4,1]{0,2,3,1:T(4,128)S(1)} %bitcast.319, f32[9,128]{1,0:T(8,128)S(1)} %eq.309), kind=kOutput, calls=%fused_computation.107.clone.1 | convolution fusion | flops 71668224 | bytes 2380320 | tf_op jit(solution)/shard_map/transpose(jvp())/while/body/eval_jaxpr/checkpoint/icku,cus->iks/dot_general | solution.py:65
  398.6 5.1 %fusion.248 = (f32[128,9,128]{2,0,1:T(8,128)S(1)}, f32[128,9,128]{2,0,1:T(8,128)S(1)}) fusion(f32[8]{0:T(128)S(1)} %iota_multiply_fusion.5, f32[128,9,128]{2,0,1:T(8,128)S(1)} %get-tuple-element.1234, f32[128,9,128]{2,0,1:T(8,128)S(1)} %get-tuple-element.1235, f32[128,8,4,1]{0,2,3,1:T(4,128)S(1)} %bitcast.319, f32[9,128]{1,0:T(8,128)S(1)} %eq.309), kind=kOutput, calls=%fused_computation.107.clone.1 | convolution fusion | flops 71668224 | bytes 2380320 | tf_op jit(solution)/shard_map/transpose(jvp())/while/body/eval_jaxpr/checkpoint/icku,cus->iks/dot_general | solution.py:65
  407.2 3.4 collective-permute-start.17
  410.5 5.2 %collective-permute-done.17 = f32[3,3,1,2,128]{4,3,2,1,0:T(2,128)S(1)} collective-permute-done((f32[3,3,1,2,128]{4,3,2,1,0:T(2,128)S(1)}, f32[3,3,1,2,128]{4,3,2,1,0:T(2,128)S(1)}, u32[]{:S(2)}, u32[]{:S(2)}) %collective-permute-start.17) | collective-permute-done | bytes 9248 | tf_op jit(solution)/shard_map/ppermute | solution.py:24
  415.8 6.9 %collective-permute-start.18 = (f32[3,3,4,1,128]{4,3,2,1,0:T(1,128)S(1)}, f32[3,3,4,1,128]{4,3,2,1,0:T(1,128)S(1)}, u32[]{:S(2)}, u32[]{:S(2)}) collective-permute-start(f32[3,3,4,1,128]{4,3,2,1,0:T(1,128)S(1)} %get-tuple-element.942), channel_id=1, source_target_pairs={{0,1},{1,2},{2,3},{3,4},{4,5},{5,6},{6,7},{7,8},{8,9},{9,10},{10,1... | collective-permute-start | bytes 55304 | tf_op jit(solution)/shard_map/ppermute | solution.py:23
  424.7 5.2 %collective-permute-done.19 = f32[3,3,4,1,128]{4,3,2,1,0:T(1,128)S(1)} collective-permute-done((f32[3,3,4,1,128]{4,3,2,1,0:T(1,128)S(1)}, f32[3,3,4,1,128]{4,3,2,1,0:T(1,128)S(1)}, u32[]{:S(2)}, u32[]{:S(2)}) %collective-permute-start.19) | collective-permute-done | bytes 18464 | tf_op jit(solution)/shard_map/ppermute | solution.py:24
  (452 shorter events, 161.6 us)
Async XLA Ops:
  0.6 57.0 %copy-start = (f32[32,256]{1,0:T(8,128)S(1)}, f32[32,256]{1,0:T(8,128)}, u32[]{:S(2)}) copy-start(f32[32,256]{1,0:T(8,128)} %param.17) | copy-start | bytes 98308
  2.7 8.0 %collective-permute-start = (f32[5,1,2,128]{3,0,2,1:T(8,128)S(1)}, f32[5,1,2,128]{3,0,2,1:T(8,128)S(1)}, u32[]{:S(2)}, u32[]{:S(2)}) collective-permute-start(f32[5,1,2,128]{3,0,2,1:T(8,128)S(1)} %get-tuple-element.982), channel_id=1, source_target_pairs={{0,16},{16,32},{32,48},{48,64},{64,80},{80,96},{96,112},{112,128},... | collective-permute-start | bytes 15368 | tf_op jit(solution)/shard_map/ppermute | solution.py:23
  8.8 8.6 %collective-permute-start.1 = (f32[5,1,2,128]{3,0,2,1:T(8,128)S(1)}, f32[5,1,2,128]{3,0,2,1:T(8,128)S(1)}, u32[]{:S(2)}, u32[]{:S(2)}) collective-permute-start(f32[5,1,2,128]{3,0,2,1:T(8,128)S(1)} %get-tuple-element.983), channel_id=1, source_target_pairs={{16,0},{32,16},{48,32},{64,48},{80,64},{96,80},{112,96},{128,112},... | collective-permute-start | bytes 15368 | tf_op jit(solution)/shard_map/ppermute | solution.py:24
  17.4 6.3 %collective-permute-start.2 = (f32[5,4,1,128]{3,0,2,1:T(8,128)S(1)}, f32[5,4,1,128]{3,0,2,1:T(8,128)S(1)}, u32[]{:S(2)}, u32[]{:S(2)}) collective-permute-start(f32[5,4,1,128]{3,0,2,1:T(8,128)S(1)} %get-tuple-element.944), channel_id=1, source_target_pairs={{0,1},{1,2},{2,3},{3,4},{4,5},{5,6},{6,7},{7,8},{8,9},{9,10},{10,1... | collective-permute-start | bytes 30728 | tf_op jit(solution)/shard_map/ppermute | solution.py:23
  21.7 7.2 %collective-permute-start.3 = (f32[5,4,1,128]{3,0,2,1:T(8,128)S(1)}, f32[5,4,1,128]{3,0,2,1:T(8,128)S(1)}, u32[]{:S(2)}, u32[]{:S(2)}) collective-permute-start(f32[5,4,1,128]{3,0,2,1:T(8,128)S(1)} %get-tuple-element.945), channel_id=1, source_target_pairs={{1,0},{2,1},{3,2},{4,3},{5,4},{6,5},{7,6},{8,7},{9,8},{10,9},{11,1... | collective-permute-start | bytes 30728 | tf_op jit(solution)/shard_map/ppermute | solution.py:24
  57.6 1.5 copy-start.13
  59.1 9.2 %collective-permute-start.4 = (f32[1,2,128,256]{3,2,1,0:T(8,128)S(1)}, f32[1,2,128,256]{3,2,1,0:T(8,128)S(1)}, u32[]{:S(2)}, u32[]{:S(2)}) collective-permute-start(f32[1,2,128,256]{3,2,1,0:T(8,128)S(1)} %get-tuple-element.930), channel_id=1, source_target_pairs={{0,16},{16,32},{32,48},{48,64},{64,80},{80,96},{96,112},{112,128},... | collective-permute-start | bytes 786440 | tf_op jit(solution)/shard_map/ppermute | solution.py:23
  61.1 14.4 %collective-permute-start.5 = (f32[1,2,128,256]{3,2,1,0:T(8,128)S(1)}, f32[1,2,128,256]{3,2,1,0:T(8,128)S(1)}, u32[]{:S(2)}, u32[]{:S(2)}) collective-permute-start(f32[1,2,128,256]{3,2,1,0:T(8,128)S(1)} %get-tuple-element.931), channel_id=1, source_target_pairs={{16,0},{32,16},{48,32},{64,48},{80,64},{96,80},{112,96},{128,112},... | collective-permute-start | bytes 786440 | tf_op jit(solution)/shard_map/ppermute | solution.py:24
  75.5 20.9 %copy-start.15 = (f32[8,256]{1,0:T(8,128)S(1)}, f32[8,256]{1,0:T(8,128)}, u32[]{:S(2)}) copy-start(f32[8,256]{1,0:T(8,128)} %param.18) | copy-start | bytes 24580
  75.5 20.9 %copy-start.16 = (bf16[256,16]{0,1:T(8,128)(2,1)S(1)}, bf16[256,16]{0,1:T(8,128)(2,1)}, u32[]{:S(2)}) copy-start(bf16[256,16]{0,1:T(8,128)(2,1)} %param.19) | copy-start | bytes 24580
  75.6 11.2 %collective-permute-start.6 = (f32[4,1,128,256]{3,2,1,0:T(8,128)S(1)}, f32[4,1,128,256]{3,2,1,0:T(8,128)S(1)}, u32[]{:S(2)}, u32[]{:S(2)}) collective-permute-start(f32[4,1,128,256]{3,2,1,0:T(8,128)S(1)} %get-tuple-element.924), channel_id=1, source_target_pairs={{0,1},{1,2},{2,3},{3,4},{4,5},{5,6},{6,7},{7,8},{8,9},{9,10},{10,1... | collective-permute-start | bytes 1572872 | tf_op jit(solution)/shard_map/ppermute | solution.py:23
  80.7 12.6 %collective-permute-start.7 = (f32[4,1,128,256]{3,2,1,0:T(8,128)S(1)}, f32[4,1,128,256]{3,2,1,0:T(8,128)S(1)}, u32[]{:S(2)}, u32[]{:S(2)}) collective-permute-start(f32[4,1,128,256]{3,2,1,0:T(8,128)S(1)} %get-tuple-element.925), channel_id=1, source_target_pairs={{1,0},{2,1},{3,2},{4,3},{5,4},{6,5},{7,6},{8,7},{9,8},{10,9},{11,1... | collective-permute-start | bytes 1572872 | tf_op jit(solution)/shard_map/ppermute | solution.py:24
  123.1 9.2 %copy-start.1 = (f32[9,128,256]{2,1,0:T(8,128)S(1)}, f32[9,128,256]{2,1,0:T(8,128)}, u32[]{:S(2)}) copy-start(f32[9,128,256]{2,1,0:T(8,128)} %get-tuple-element.1221) | copy-start | bytes 3538948 | tf_op jit(solution)/shard_map/transpose(jvp())/while
  161.4 9.2 %copy-start.1 = (f32[9,128,256]{2,1,0:T(8,128)S(1)}, f32[9,128,256]{2,1,0:T(8,128)}, u32[]{:S(2)}) copy-start(f32[9,128,256]{2,1,0:T(8,128)} %get-tuple-element.1221) | copy-start | bytes 3538948 | tf_op jit(solution)/shard_map/transpose(jvp())/while
  199.7 9.2 %copy-start.1 = (f32[9,128,256]{2,1,0:T(8,128)S(1)}, f32[9,128,256]{2,1,0:T(8,128)}, u32[]{:S(2)}) copy-start(f32[9,128,256]{2,1,0:T(8,128)} %get-tuple-element.1221) | copy-start | bytes 3538948 | tf_op jit(solution)/shard_map/transpose(jvp())/while
  238.1 9.2 %copy-start.1 = (f32[9,128,256]{2,1,0:T(8,128)S(1)}, f32[9,128,256]{2,1,0:T(8,128)}, u32[]{:S(2)}) copy-start(f32[9,128,256]{2,1,0:T(8,128)} %get-tuple-element.1221) | copy-start | bytes 3538948 | tf_op jit(solution)/shard_map/transpose(jvp())/while
  253.2 46.3 %copy-start.3 = (f32[1,2,2,128,256]{4,3,2,1,0:T(8,128)}, f32[1,2,2,128,256]{4,3,2,1,0:T(8,128)S(1)}, u32[]{:S(2)}) copy-start(f32[1,2,2,128,256]{4,3,2,1,0:T(8,128)S(1)} %get-tuple-element.986) | copy-start | bytes 1572868
  253.2 46.3 %copy-start.5 = (f32[1,2,2,128,256]{4,3,2,1,0:T(8,128)}, f32[1,2,2,128,256]{4,3,2,1,0:T(8,128)S(1)}, u32[]{:S(2)}) copy-start(f32[1,2,2,128,256]{4,3,2,1,0:T(8,128)S(1)} %get-tuple-element.987) | copy-start | bytes 1572868
  253.2 46.3 %copy-start.7 = (f32[1,2,2,128,256]{4,3,2,1,0:T(8,128)}, f32[1,2,2,128,256]{4,3,2,1,0:T(8,128)S(1)}, u32[]{:S(2)}) copy-start(f32[1,2,2,128,256]{4,3,2,1,0:T(8,128)S(1)} %maximum_bitcast_fusion.5) | copy-start | bytes 1572868
  254.8 44.6 %collective-permute-start.12 = (f32[3,1,2,128,256]{4,3,2,1,0:T(8,128)}, f32[3,1,2,128,256]{4,3,2,1,0:T(8,128)S(1)}, u32[]{:S(2)}, u32[]{:S(2)}) collective-permute-start(f32[3,1,2,128,256]{4,3,2,1,0:T(8,128)} %get-tuple-element.920), channel_id=1, source_target_pairs={{0,16},{16,32},{32,48},{48,64},{64,80},{80,96},{96,112},{112,128},... | collective-permute-start | bytes 2359304 | tf_op jit(solution)/shard_map/ppermute | solution.py:23
  256.7 42.7 %collective-permute-start.13 = (f32[3,1,2,128,256]{4,3,2,1,0:T(8,128)}, f32[3,1,2,128,256]{4,3,2,1,0:T(8,128)S(1)}, u32[]{:S(2)}, u32[]{:S(2)}) collective-permute-start(f32[3,1,2,128,256]{4,3,2,1,0:T(8,128)} %get-tuple-element.921), channel_id=1, source_target_pairs={{16,0},{32,16},{48,32},{64,48},{80,64},{96,80},{112,96},{128,112},... | collective-permute-start | bytes 2359304 | tf_op jit(solution)/shard_map/ppermute | solution.py:24
  260.2 17.6 %collective-permute-start.8 = (f32[3,3,1,2,128]{4,3,2,1,0:T(2,128)S(1)}, f32[3,3,1,2,128]{4,3,2,1,0:T(2,128)S(1)}, u32[]{:S(2)}, u32[]{:S(2)}) collective-permute-start(f32[3,3,1,2,128]{4,3,2,1,0:T(2,128)S(1)} %get-tuple-element.978), channel_id=1, source_target_pairs={{0,16},{16,32},{32,48},{48,64},{64,80},{80,96},{96,112},{112,128},... | collective-permute-start | bytes 27656 | tf_op jit(solution)/shard_map/ppermute | solution.py:23
  266.3 18.1 %collective-permute-start.9 = (f32[3,3,1,2,128]{4,3,2,1,0:T(2,128)S(1)}, f32[3,3,1,2,128]{4,3,2,1,0:T(2,128)S(1)}, u32[]{:S(2)}, u32[]{:S(2)}) collective-permute-start(f32[3,3,1,2,128]{4,3,2,1,0:T(2,128)S(1)} %get-tuple-element.979), channel_id=1, source_target_pairs={{16,0},{32,16},{48,32},{64,48},{80,64},{96,80},{112,96},{128,112},... | collective-permute-start | bytes 27656 | tf_op jit(solution)/shard_map/ppermute | solution.py:24
  284.5 69.9 %collective-permute-start.10 = (f32[3,3,4,1,128]{4,3,2,1,0:T(1,128)S(1)}, f32[3,3,4,1,128]{4,3,2,1,0:T(1,128)S(1)}, u32[]{:S(2)}, u32[]{:S(2)}) collective-permute-start(f32[3,3,4,1,128]{4,3,2,1,0:T(1,128)S(1)} %get-tuple-element.940), channel_id=1, source_target_pairs={{0,1},{1,2},{2,3},{3,4},{4,5},{5,6},{6,7},{7,8},{8,9},{9,10},{10,1... | collective-permute-start | bytes 55304 | tf_op jit(solution)/shard_map/ppermute | solution.py:23
  297.3 57.2 %collective-permute-start.11 = (f32[3,3,4,1,128]{4,3,2,1,0:T(1,128)S(1)}, f32[3,3,4,1,128]{4,3,2,1,0:T(1,128)S(1)}, u32[]{:S(2)}, u32[]{:S(2)}) collective-permute-start(f32[3,3,4,1,128]{4,3,2,1,0:T(1,128)S(1)} %get-tuple-element.941), channel_id=1, source_target_pairs={{1,0},{2,1},{3,2},{4,3},{5,4},{6,5},{7,6},{8,7},{9,8},{10,9},{11,1... | collective-permute-start | bytes 55304 | tf_op jit(solution)/shard_map/ppermute | solution.py:24
  299.4 0.9 copy-start.9
  300.3 2.1 copy-start.11
  300.5 10.2 %copy-start.2 = (f32[4,4,128,256]{3,2,1,0:T(8,128)S(1)}, f32[4,4,128,256]{3,2,1,0:T(8,128)}, u32[]{:S(2)}) copy-start(f32[4,4,128,256]{3,2,1,0:T(8,128)} %get-tuple-element.1449) | copy-start | bytes 6291460
  302.4 52.1 %collective-permute-start.14 = (f32[3,4,1,128,256]{4,3,2,1,0:T(8,128)}, f32[3,4,1,128,256]{4,3,2,1,0:T(8,128)}, u32[]{:S(2)}, u32[]{:S(2)}) collective-permute-start(f32[3,4,1,128,256]{4,3,2,1,0:T(8,128)} %get-tuple-element.908), channel_id=1, source_target_pairs={{0,1},{1,2},{2,3},{3,4},{4,5},{5,6},{6,7},{7,8},{8,9},{9,10},{10,1... | collective-permute-start | bytes 4718600 | tf_op jit(solution)/shard_map/ppermute | solution.py:23
  308.2 46.4 %collective-permute-start.15 = (f32[3,4,1,128,256]{4,3,2,1,0:T(8,128)}, f32[3,4,1,128,256]{4,3,2,1,0:T(8,128)}, u32[]{:S(2)}, u32[]{:S(2)}) collective-permute-start(f32[3,4,1,128,256]{4,3,2,1,0:T(8,128)} %get-tuple-element.909), channel_id=1, source_target_pairs={{1,0},{2,1},{3,2},{4,3},{5,4},{6,5},{7,6},{8,7},{9,8},{10,9},{11,1... | collective-permute-start | bytes 4718600 | tf_op jit(solution)/shard_map/ppermute | solution.py:24
  354.4 1.8 copy-start.4
  354.4 1.8 copy-start.6
  354.4 1.8 copy-start.8
  354.4 2.0 copy-start.10
  354.4 2.2 copy-start.12
  360.0 1.0 copy-start.17
  360.1 2.9 copy-start.14
  405.2 5.3 %collective-permute-start.16 = (f32[3,3,1,2,128]{4,3,2,1,0:T(2,128)S(1)}, f32[3,3,1,2,128]{4,3,2,1,0:T(2,128)S(1)}, u32[]{:S(2)}, u32[]{:S(2)}) collective-permute-start(f32[3,3,1,2,128]{4,3,2,1,0:T(2,128)S(1)} %get-tuple-element.980), channel_id=1, source_target_pairs={{0,16},{16,32},{32,48},{48,64},{64,80},{80,96},{96,112},{112,128},... | collective-permute-start | bytes 27656 | tf_op jit(solution)/shard_map/ppermute | solution.py:23
  407.2 8.6 %collective-permute-start.17 = (f32[3,3,1,2,128]{4,3,2,1,0:T(2,128)S(1)}, f32[3,3,1,2,128]{4,3,2,1,0:T(2,128)S(1)}, u32[]{:S(2)}, u32[]{:S(2)}) collective-permute-start(f32[3,3,1,2,128]{4,3,2,1,0:T(2,128)S(1)} %get-tuple-element.981), channel_id=1, source_target_pairs={{16,0},{32,16},{48,32},{64,48},{80,64},{96,80},{112,96},{128,112},... | collective-permute-start | bytes 27656 | tf_op jit(solution)/shard_map/ppermute | solution.py:24
  415.8 8.9 %collective-permute-start.18 = (f32[3,3,4,1,128]{4,3,2,1,0:T(1,128)S(1)}, f32[3,3,4,1,128]{4,3,2,1,0:T(1,128)S(1)}, u32[]{:S(2)}, u32[]{:S(2)}) collective-permute-start(f32[3,3,4,1,128]{4,3,2,1,0:T(1,128)S(1)} %get-tuple-element.942), channel_id=1, source_target_pairs={{0,1},{1,2},{2,3},{3,4},{4,5},{5,6},{6,7},{7,8},{8,9},{9,10},{10,1... | collective-permute-start | bytes 55304 | tf_op jit(solution)/shard_map/ppermute | solution.py:23
  422.8 7.2 %collective-permute-start.19 = (f32[3,3,4,1,128]{4,3,2,1,0:T(1,128)S(1)}, f32[3,3,4,1,128]{4,3,2,1,0:T(1,128)S(1)}, u32[]{:S(2)}, u32[]{:S(2)}) collective-permute-start(f32[3,3,4,1,128]{4,3,2,1,0:T(1,128)S(1)} %get-tuple-element.943), channel_id=1, source_target_pairs={{1,0},{2,1},{3,2},{4,3},{5,4},{6,5},{7,6},{8,7},{9,8},{10,9},{11,1... | collective-permute-start | bytes 55304 | tf_op jit(solution)/shard_map/ppermute | solution.py:24
where the time goes:
time: 434 us; the launch traced here: 431 us
  matrix products  87.6 us (20%)
  other arithmetic  85.2 us (20%)
  starting transfers between devices  76.7 us (18%)
  local copies, waits for them, and re-layouts  75.7 us (17%)
  waiting for transfers between devices  60 us (14%)
  loops' own time  44.1 us (10%)
    ppermute x10, starting transfers between devices, extended(): before = lax.ppermute(last, axis, up)  52.8 us
    ppermute x10, waiting for transfers between devices, extended(): after = lax.ppermute(first, axis, down)  42.6 us
    dot_general x12, matrix products, cell_energy(): message = jnp.dot(radial_basis, scaled, preferred_element_type=jnp.float32)  33.6 us
    dot_general x8, matrix products, density_block(): jnp.einsum('icku,cus->iks', radial_basis, onehot, precision=lax.Precision...  33.2 us
    convert_element_type x4, local copies, waits for them, and re-layouts, cell_energy(): pair_basis(near_pos, near_valid).astype(jnp.bfloat16)  24.2 us
    ppermute x10, starting transfers between devices, extended(): after = lax.ppermute(first, axis, down)  23.9 us
    another operation x2, loops' own time, layer_two(): lax.map(jax.checkpoint(layer_one_cell), jnp.arange(span_x * span_y, dtype...  22.6 us
    another operation x2, loops' own time, cell_densities(): lax.map(jax.checkpoint(cell_one_cell), jnp.arange(span_x * span_y, dtype=...  21.5 us
  transfers between devices with their start and end apart: 20, of which 10 were waited for; matrix products, arithmetic and copies ran while one was open for 8% of the time, Pallas kernels for 0%

commit v1 on v0

v1 whole, which is shorter than its diff:
```python
import functools
import math

import jax
import jax.numpy as jnp
from jax import lax
from jax.experimental import pallas as pl
from jax.experimental.pallas import tpu as pltpu
from jax.sharding import PartitionSpec as P

MESH = pl.DeviceIdType.MESH
F32 = jnp.float32
BF16 = jnp.bfloat16

RADIAL = 8
SPECIES = 4
N = 128
CH = 256
CUT = 6.0
SOFT = 0.01
SPACE = CUT / (RADIAL - 1)
COEF = [math.exp(8.0 * k - k * k) for k in range(RADIAL)]
DIRS = [(dx, dy) for dx in (-1, 0, 1) for dy in (-1, 0, 1) if (dx, dy) != (0, 0)]
OWN = 4 * N
HALO = 5 * N
ROWS = 32
BLOCKS = N // ROWS


def nn(a, b):
    return lax.dot_general(a, b, (((1,), (0,)), ((), ())), preferred_element_type=F32)


def nt(a, b):
    return lax.dot_general(a, b, (((1,), (1,)), ((), ())), preferred_element_type=F32)


def border(d):
    return {1: 2, -1: 1, 0: pl.ds(1, 2)}[d]


def landing(d):
    return {1: 0, -1: 3, 0: pl.ds(1, 2)}[d]


def beyond(d):
    return {1: 3, -1: 0, 0: pl.ds(1, 2)}[d]


def own_slot(c):
    return 1 + c // 2, 1 + c % 2


def halo_slots(c):
    a_out, b_out = 3 * (c // 2), 3 * (c % 2)
    return [(a_out, b_out), (a_out, 1), (a_out, 2), (1, b_out), (2, b_out)]


def sigmoid(x):
    return 1.0 / (1.0 + jnp.exp(-x))


def kernel(
    nx, ny,
    pos_ref, valid_ref, spec_ref, table_ref, gain_ref, readout_ref,
    forces_ref, energies_ref,
    atoms, xi, basis, u_s, a_s, rc_s, ri_s, dens, hid_t, hid, hid_own, slope,
    msg, gms, gms_t, gm_t, g1, onehot, tab_t, tab_s, gk, gk_t, read_t,
    gpart, grecv, gsum, fi, fj, fpart, frecv, gs,
    send_sem, recv_sem,
):
    gx, gy = lax.axis_index("gx"), lax.axis_index("gy")

    def there(dx, dy):
        ok = None
        for d, g, n in ((dx, gx, nx), (dy, gy, ny)):
            if d:
                one = (g < n - 1) if d > 0 else (g > 0)
                ok = one if ok is None else jnp.logical_and(ok, one)
        return ok

    def copy(r, n, src, dst, peer):
        return pltpu.make_async_remote_copy(
            src_ref=src, dst_ref=dst, send_sem=send_sem.at[r, n], recv_sem=recv_sem.at[r, n],
            device_id=peer, device_id_type=MESH,
        )

    def outward(r, buf, wait):
        for n, (dx, dy) in enumerate(DIRS):
            src = buf.at[border(dx), border(dy)]
            dst = buf.at[landing(dx), landing(dy)]
            if wait == "recv":
                @pl.when(there(-dx, -dy))
                def _():
                    copy(r, n, src, dst, (gx - dx, gy - dy)).wait_recv()
            else:
                @pl.when(there(dx, dy))
                def _():
                    c = copy(r, n, src, dst, (gx + dx, gy + dy))
                    c.start() if wait == "start" else c.wait_send()

    def inward(r, buf, land, wait):
        for n, (dx, dy) in enumerate(DIRS):
            src = buf.at[beyond(dx), beyond(dy)]
            dst = land.at[n, 0] if dx and dy else land.at[n]
            if wait == "recv":
                @pl.when(there(-dx, -dy))
                def _():
                    copy(r, n, src, dst, (gx - dx, gy - dy)).wait_recv()
            else:
                @pl.when(there(dx, dy))
                def _():
                    c = copy(r, n, src, dst, (gx + dx, gy + dy))
                    c.start() if wait == "start" else c.wait_send()

    def returned(land, a, b):
        total = None
        for n, (dx, dy) in enumerate(DIRS):
            if (dx == 0 or a == (1 if dx == 1 else 2)) and (dy == 0 or b == (1 if dy == 1 else 2)):
                m = a - 1 if dx == 0 else (b - 1 if dy == 0 else 0)
                total = land[n, m] if total is None else total + land[n, m]
        return total

    for a in range(4):
        for b in range(4):
            if a in (1, 2) and b in (1, 2):
                rows = [pos_ref[i, a - 1, b - 1 : b, :] for i in range(3)]
                rows.append(valid_ref[a - 1, b - 1 : b, :].astype(F32))
                rows.append(spec_ref[a - 1, b - 1 : b, :].astype(F32))
                rows.append(jnp.zeros((3, N), F32))
                atoms[a, b] = jnp.concatenate(rows, 0)
            else:
                atoms[a, b] = jnp.zeros((8, N), F32)
                dens[a, b] = jnp.zeros((RADIAL * SPECIES, N), F32)
    grecv[...] = jnp.zeros_like(grecv)
    frecv[...] = jnp.zeros_like(frecv)

    barrier = pltpu.get_barrier_semaphore()
    for dx, dy in DIRS:
        @pl.when(there(dx, dy))
        def _():
            pl.semaphore_signal(barrier, inc=1, device_id=(gx + dx, gy + dy), device_id_type=MESH)
    span_x = 1 + jnp.where(gx > 0, 1, 0) + jnp.where(gx < nx - 1, 1, 0)
    span_y = 1 + jnp.where(gy > 0, 1, 0) + jnp.where(gy < ny - 1, 1, 0)

    table = table_ref[...] * 0.125
    high = table.astype(BF16).astype(F32)
    low = table - high
    tab_s[...] = jnp.concatenate([high, low], 0).astype(BF16)
    stacked = jnp.concatenate([high, high, low, jnp.zeros((32, CH), F32)], 0)
    tab_t[...] = stacked.T.astype(BF16)
    for k in range(RADIAL):
        row = gain_ref[k : k + 1, :] * (COEF[k] / 32.0)
        gk[k] = row
        gk_t[k] = jnp.broadcast_to(row, (N, CH)).T
    readout_f = jnp.concatenate([readout_ref[...].astype(F32), jnp.zeros((CH, N - 16), F32)], 1)
    read_t[...] = readout_f.T.astype(BF16)
    for c in range(4):
        a, b = own_slot(c)
        tile = atoms[a, b]
        x = jnp.where(tile[3:4] > 0.0, tile[0:1], 1e4)
        xi[c, 0] = jnp.broadcast_to(x, (N, N)).T
        xi[c, 1] = jnp.broadcast_to(tile[1:2], (N, N)).T
        xi[c, 2] = jnp.broadcast_to(tile[2:3], (N, N)).T

    pl.semaphore_wait(barrier, span_x * span_y - 1)
    outward(0, atoms, "start")

    def offsets(c, rows, a, b):
        xj = jnp.where(atoms[a, b, 3:4, :] > 0.0, atoms[a, b, 0:1, :], -1e4)
        dx = xi[c, 0, rows, :] - xj
        dy = xi[c, 1, rows, :] - atoms[a, b, 1:2, :]
        dz = xi[c, 2, rows, :] - atoms[a, b, 2:3, :]
        return dx, dy, dz

    def pair_basis(c, block, a, b, lane, self_cell):
        rows = pl.ds(block * ROWS, ROWS)
        cols = slice(lane, lane + N)
        dx, dy, dz = offsets(c, rows, a, b)
        sq = dx * dx + dy * dy + (dz * dz + SOFT)
        if self_cell is not None:
            i = lax.broadcasted_iota(jnp.int32, (ROWS, N), 0) + block * ROWS
            j = lax.broadcasted_iota(jnp.int32, (ROWS, N), 1)
            sq = jnp.where(jnp.logical_and(i == j, self_cell), 1e8, sq)
        ri = lax.rsqrt(sq)
        reach = jnp.maximum(1.0 - sq * (1.0 / (CUT * CUT)), 0.0)
        t = jnp.minimum(sq * ri * (1.0 / SPACE), float(RADIAL - 1))
        u = jnp.exp(2.0 * t - 8.0)
        amp = jnp.exp(-(t * t)) * reach
        u_s[c, rows, cols] = u
        a_s[c, rows, cols] = amp
        rc_s[c, rows, cols] = reach
        ri_s[c, rows, cols] = ri
        term = amp * reach
        for k in range(RADIAL):
            basis[c, pl.ds(k * N + block * ROWS, ROWS), cols] = term.astype(BF16)
            if k < RADIAL - 1:
                term = term * u

    def own_pairs(step, carry):
        c, block = step // BLOCKS, step % BLOCKS
        for j in range(4):
            a, b = own_slot(j)
            pair_basis(c, block, a, b, j * N, c == j)
        return carry

    def halo_pairs(step, carry):
        c, block = step // BLOCKS, step % BLOCKS
        for m, (a, b) in enumerate(halo_slots(c)):
            pair_basis(c, block, a, b, OWN + m * N, None)
        return carry

    lax.fori_loop(0, 4 * BLOCKS, own_pairs, 0)
    outward(0, atoms, "recv")
    for a in range(4):
        for b in range(4):
            kind = atoms[a, b, 4:5, :].astype(jnp.int32)
            r = lax.broadcasted_iota(jnp.int32, (N, N), 0)
            hit = jnp.logical_and(r < 64, (r & 3) == kind)
            onehot[a, b] = jnp.where(hit, 1.0, 0.0).astype(BF16)
    lax.fori_loop(0, 4 * BLOCKS, halo_pairs, 0)

    def kinds(a, b):
        kind = atoms[a, b, 4:5, :].astype(jnp.int32)
        r = lax.broadcasted_iota(jnp.int32, (16, N), 0)
        return jnp.where(r == kind, 1.0, 0.0).astype(BF16)

    def densities(c, carry):
        cells = [own_slot(j) for j in range(4)] + halo_slots(c)
        hot = jnp.concatenate([kinds(a, b) for a, b in cells], 1)
        out = nt(hot, basis[c])
        a, b = own_slot(c)
        for k in range(RADIAL):
            dens[a, b, k * SPECIES : (k + 1) * SPECIES, :] = (
                out[0:SPECIES, k * N : (k + 1) * N] * COEF[k]
            )
        return carry

    lax.fori_loop(0, 4, densities, 0)
    outward(1, dens, "start")

    def features(a, b):
        d = dens[a, b]
        top = d.astype(BF16)
        rest = (d - top.astype(F32)).astype(BF16)
        cat = jnp.concatenate([top, rest, top, jnp.zeros((32, N), BF16)], 0)
        z = nn(tab_t[...], cat)
        s = sigmoid(z)
        h = z * s
        hid_t[a, b] = h.astype(BF16)
        slope[a, b] = s * (1.0 + z * (1.0 - s))
        return h.T

    def own_features(c, carry):
        a, b = own_slot(c)
        h = features(a, b)
        hid_own[c] = h
        hid[a, b] = h.astype(BF16)
        return carry

    lax.fori_loop(0, 4, own_features, 0)

    def gained(prod):
        total = prod[0:N] * gk[0]
        for k in range(1, RADIAL):
            total = total + prod[k * N : (k + 1) * N] * gk[k]
        return total

    def own_message(c, carry):
        h = jnp.concatenate([hid[a, b] for a, b in [own_slot(j) for j in range(4)]], 0)
        msg[c] = gained(nn(basis[c, :, 0:OWN], h))
        return carry

    lax.fori_loop(0, 4, own_message, 0)
    outward(1, dens, "recv")

    def halo_features(step, carry):
        q = step - 8
        a = jnp.where(step < 8, 3 * (step // 4), 1 + q // 2)
        b = jnp.where(step < 8, step % 4, 3 * (q % 2))
        hid[a, b] = features(a, b).astype(BF16)
        return carry

    lax.fori_loop(0, 12, halo_features, 0)

    def second_layer(c, carry):
        a, b = own_slot(c)
        h = jnp.concatenate([hid[p, q] for p, q in halo_slots(c)], 0)
        m = msg[c] + gained(nn(basis[c, :, OWN:], h))
        p = m + hid_own[c]
        s = sigmoid(p)
        second = (p * s).astype(BF16)
        heads = nt(read_t[...], second)
        valid = atoms[a, b, 3:4, :]
        sh = sigmoid(heads)
        energies_ref[a - 1, b - 1] = (valid * (heads * sh))[0:16]
        back = (valid * (1.0 / 16.0)) * (sh * (1.0 + heads * (1.0 - sh)))
        dsec = nn(back.T.astype(BF16), read_t[...]).astype(BF16).astype(F32)
        gm = dsec * (s * (1.0 + p * (1.0 - s)))
        gmt = gm.T
        gm_t[c] = gmt
        for k in range(RADIAL):
            gms[c, k * N : (k + 1) * N, :] = (gm * gk[k]).astype(BF16)
            gms_t[c, :, k * N : (k + 1) * N] = (gmt * gk_t[k]).astype(BF16)
        return carry

    lax.fori_loop(0, 4, second_layer, 0)

    gpart[...] = jnp.zeros_like(gpart)

    def project(x):
        out = nn(tab_s[...], x.astype(BF16))
        return out[0:32] + out[32:64]

    def halo_grad(c, carry):
        x = nn(gms_t[c], basis[c, :, OWN:])
        for m, (a, b) in enumerate(halo_slots(c)):
            gpart[a, b] += project(x[:, m * N : (m + 1) * N] * slope[a, b])
        return carry

    lax.fori_loop(0, 4, halo_grad, 0)
    inward(2, gpart, grecv, "start")

    def own_grad(j, carry):
        a, b = own_slot(j)
        cols = pl.ds(pl.multiple_of(j * N, N), N)
        x = gm_t[j]
        for c in range(4):
            x = x + nn(gms_t[c], basis[c, :, cols])
        gsum[j] = project(x * slope[a, b])
        return carry

    lax.fori_loop(0, 4, own_grad, 0)
    inward(2, gpart, grecv, "recv")

    for c in range(4):
        a, b = own_slot(c)
        g = gsum[c] + returned(grecv, a, b)
        r = lax.broadcasted_iota(jnp.int32, (32, N), 0) >> 2
        coef = jnp.full((32, N), COEF[0], F32)
        for k in range(1, RADIAL):
            coef = jnp.where(r == k, COEF[k], coef)
        g = g * coef
        top = g.astype(BF16).astype(F32)
        gt = jnp.concatenate([top, g - top, jnp.zeros((64, N), F32)], 0).T
        lane = lax.broadcasted_iota(jnp.int32, (N, N), 1)
        for k in range(RADIAL):
            keep = jnp.logical_and(lane < 64, ((lane & 31) >> 2) == k)
            g1[c, k * N : (k + 1) * N, :] = jnp.where(keep, gt, 0.0).astype(BF16)

    fi[...] = jnp.zeros_like(fi)
    fj[...] = jnp.zeros_like(fj)

    def pair_forces(c, cells, lane0):
        h = jnp.concatenate([hid_t[a, b] for a, b in cells], 1)
        o = jnp.concatenate([onehot[a, b] for a, b in cells], 1)
        width = len(cells) * N
        gs[:, 0:width] = nn(gms[c], h) + nn(g1[c], o)

        def body(block, carry):
            rows = pl.ds(block * ROWS, ROWS)
            sums = [jnp.zeros((ROWS, N), F32) for _ in range(3)]
            for m, (a, b) in enumerate(cells):
                cols = slice(lane0 + m * N, lane0 + (m + 1) * N)
                u = u_s[c, rows, cols]

                def grad(k):
                    return gs[pl.ds(k * N + block * ROWS, ROWS), m * N : (m + 1) * N]

                poly = grad(RADIAL - 1)
                slant = poly
                for k in range(RADIAL - 2, -1, -1):
                    poly = poly * u + grad(k)
                    if k:
                        slant = slant * u + poly
                slant = slant * u
                reach = rc_s[c, rows, cols]
                inner = ri_s[c, rows, cols] * slant * (2.0 / SPACE) - poly * (2.0 / SPACE**2)
                force = a_s[c, rows, cols] * (reach * inner - poly * (4.0 / CUT**2))
                for i, d in enumerate(offsets(c, rows, a, b)):
                    f = force * d
                    sums[i] = sums[i] + f
                    part = f[0:8]
                    for q in range(1, ROWS // 8):
                        part = part + f[8 * q : 8 * q + 8]
                    fj[a, b, i] += part
            for i in range(3):
                fi[c, i, rows, :] += sums[i]
            return carry

        lax.fori_loop(0, BLOCKS, body, 0)

    def halo_forces(c, carry):
        pair_forces(c, halo_slots(c), OWN)
        return carry

    def own_forces(c, carry):
        pair_forces(c, [own_slot(j) for j in range(4)], 0)
        return carry

    lax.fori_loop(0, 4, halo_forces, 0)
    for a in range(4):
        for b in range(4):
            if not (a in (1, 2) and b in (1, 2)):
                rows = [jnp.sum(fj[a, b, i], 0, keepdims=True) for i in range(3)]
                fpart[a, b] = jnp.concatenate(rows + [jnp.zeros((5, N), F32)], 0)
    inward(3, fpart, frecv, "start")
    lax.fori_loop(0, 4, own_forces, 0)
    sums = []
    for c in range(4):
        a, b = own_slot(c)
        rows = []
        for i in range(3):
            mine = jnp.sum(fi[c, i].T, 0, keepdims=True)
            rows.append(jnp.sum(fj[a, b, i], 0, keepdims=True) - mine)
        sums.append(jnp.concatenate(rows + [jnp.zeros((5, N), F32)], 0))
    inward(3, fpart, frecv, "recv")
    for c in range(4):
        a, b = own_slot(c)
        forces_ref[a - 1, b - 1] = sums[c] + returned(frecv, a, b)
    outward(0, atoms, "send")
    outward(1, dens, "send")
    inward(2, gpart, grecv, "send")
    inward(3, fpart, frecv, "send")


def shards(nx, ny, positions, valid_mask, species, density_table, radial_gain, readout):
    vmem = pltpu.VMEM
    whole = pl.BlockSpec(memory_space=pltpu.VMEM)
    wide = OWN + HALO
    forces, energies = pl.pallas_call(
        functools.partial(kernel, nx, ny),
        out_shape=(
            jax.ShapeDtypeStruct((2, 2, 8, N), F32),
            jax.ShapeDtypeStruct((2, 2, 16, N), F32),
        ),
        in_specs=[whole] * 6,
        out_specs=(whole, whole),
        scratch_shapes=[
            vmem((4, 4, 8, N), F32),
            vmem((4, 3, N, N), F32),
            vmem((4, RADIAL * N, wide), BF16),
            vmem((4, N, wide), F32),
            vmem((4, N, wide), F32),
            vmem((4, N, wide), F32),
            vmem((4, N, wide), F32),
            vmem((4, 4, RADIAL * SPECIES, N), F32),
            vmem((4, 4, CH, N), BF16),
            vmem((4, 4, N, CH), BF16),
            vmem((4, N, CH), F32),
            vmem((4, 4, CH, N), F32),
            vmem((4, N, CH), F32),
            vmem((4, RADIAL * N, CH), BF16),
            vmem((4, CH, RADIAL * N), BF16),
            vmem((4, CH, N), F32),
            vmem((4, RADIAL * N, N), BF16),
            vmem((4, 4, N, N), BF16),
            vmem((CH, N), BF16),
            vmem((64, CH), BF16),
            vmem((RADIAL, 1, CH), F32),
            vmem((RADIAL, CH, N), F32),
            vmem((N, CH), BF16),
            vmem((4, 4, 32, N), F32),
            vmem((8, 2, 32, N), F32),
            vmem((4, 32, N), F32),
            vmem((4, 3, N, N), F32),
            vmem((4, 4, 3, 8, N), F32),
            vmem((4, 4, 8, N), F32),
            vmem((8, 2, 8, N), F32),
            vmem((RADIAL * N, HALO), F32),
            pltpu.SemaphoreType.DMA((4, 8)),
            pltpu.SemaphoreType.DMA((4, 8)),
        ],
        compiler_params=pltpu.CompilerParams(
            collective_id=0, has_side_effects=True, vmem_limit_bytes=56 * 1024 * 1024
        ),
    )(positions, valid_mask, species, density_table, radial_gain, readout)
    return forces[:, :, :3].transpose(2, 0, 1, 3), energies.transpose(2, 0, 1, 3)


def solution(mesh):
    nx, ny = mesh.shape["gx"], mesh.shape["gy"]
    in_specs = (P(None, "gx", "gy", None), P("gx", "gy", None), P("gx", "gy", None), P(), P(), P())
    out_specs = (P(None, "gx", "gy", None), P(None, "gx", "gy", None))
    return jax.shard_map(
        functools.partial(shards, nx, ny), mesh=mesh, in_specs=in_specs, out_specs=out_specs,
        check_vma=False,
    )
```

time: 434 us -> 59.1 us (0.14)
  matrix products: 87.6 us -> 0 us
  other arithmetic: 85.2 us -> 0 us
  starting transfers between devices: 76.7 us -> 0 us
  local copies, waits for them, and re-layouts: 75.7 us -> 3.37 us
  waiting for transfers between devices: 60 us -> 0 us
  Pallas kernels: 0 us -> 54.8 us
  loops' own time: 44.1 us -> 0 us
    dot_general x30 -> x0, matrix products: 87.6 us -> none  [the longest x12 33.6 us: cell_energy(): message = jnp.dot(radial_basis, scaled, preferred_element_type=jnp.float32)]
    ppermute x20 -> x0, starting transfers between devices: 76.7 us -> none  [the longest x10 52.8 us: extended(): before = lax.ppermute(last, axis, up)]
    ppermute x20 -> x0, waiting for transfers between devices: 60 us -> none  [the longest x10 42.6 us: extended(): after = lax.ppermute(first, axis, down)]
    pallas_call x0 -> x1, Pallas kernels: none -> 54.8 us  [shards(): pl.pallas_call(functools.partial(kernel, nx, ny), out_shape=(jax.ShapeDty...]
    another operation x4 -> x0, loops' own time: 44.1 us -> none  [the longest x2 22.6 us: layer_two(): lax.map(jax.checkpoint(layer_one_cell), jnp.arange(span_x * span_y, dtype...]
    reduce_sum x32 -> x0, other arithmetic: 39.8 us -> none  [the longest x4 20.9 us: pair_basis(): return weight[:, :, None, :] * gaussian]
    convert_element_type x4 -> x0, local copies, waits for them, and re-layouts: 24.2 us -> none  [cell_energy(): pair_basis(near_pos, near_valid).astype(jnp.bfloat16)]
    dynamic_slice x56 -> x0, local copies, waits for them, and re-layouts: 19 us -> none  [the longest x16 12.7 us: cell_densities(): lax.map(jax.checkpoint(cell_one_cell), jnp.arange(span_x * span_y, dtype=...]
  transfers between devices with their start and end apart: 20 -> 0, of which waited for: 10 -> 0; matrix products, arithmetic and copies ran while one was open for 8% -> 0% of each run, Pallas kernels for 0% -> 0%
where the time goes in v1:
time: 59.1 us; the launch traced here: 58.9 us
  Pallas kernels  54.8 us (93%)
  local copies, waits for them, and re-layouts  3.37 us (6%)
  between operations  0.65 us (1%)
    pallas_call x1, Pallas kernels, shards(): pl.pallas_call(functools.partial(kernel, nx, ny), out_shape=(jax.ShapeDty...  54.8 us
    unnamed x5, local copies, waits for them, and re-layouts  2.65 us

profile of v1, /device:TPU:95, one launch (start us, length us, event | category | flops | bytes accessed | tf_op | source)
XLA Modules:
  0.0 58.9 jit_solution(14584280825626277027)
XLA Ops:
  0.6 1.4 %copy.8.readout_ref = bf16[256,16]{1,0:T(8,128)(2,1)} copy(bf16[256,16]{0,1:T(8,128)(2,1)} %param.11) | data formatting | bytes 16384 | tf_op args[5]
  2.0 54.8 %shard_map.77 = (f32[2,2,8,128]{3,2,1,0:T(8,128)}, f32[2,2,16,128]{3,2,1,0:T(8,128)}) custom-call(f32[3,2,2,128]{3,2,1,0:T(2,128)} %pos_ref.1, s32[2,2,128]{2,1,0:T(2,128)} %valid_ref.1, s32[2,2,128]{2,1,0:T(2,128)} %spec_ref.1, f32[32,256]{1,0:T(8,128)} %table_ref.1, f32[8,256]{1,0:T(8,128)} %gain_ref.1, bf16[256,16]{1,0:T(8,128)(2,1)} %copy.8.readout_ref), custom_call_target="tpu_custom_call" | custom-call | tf_op jit(solution)/shard_map/pallas_call | solution.py:431
  56.9 0.0 copy-start
  56.9 0.7 %slice_bitcast_fusion = f32[3,2,2,128]{3,0,2,1:T(4,128)S(1)} fusion(f32[2,2,8,128]{3,2,1,0:T(8,128)} %get-tuple-element.4), kind=kLoop, calls=%fused_computation | loop fusion | bytes 12288 | tf_op jit(solution)/shard_map/transpose | solution.py:478
  57.6 0.6 %copy.9 = f32[3,2,2,128]{3,2,1,0:T(2,128)} copy(f32[3,2,2,128]{3,0,2,1:T(4,128)S(1)} %slice_bitcast_fusion) | data formatting | bytes 12288
  58.2 0.0 copy-done
  58.2 0.6 %copy.10 = f32[16,2,2,128]{3,2,1,0:T(2,128)} copy(f32[16,2,2,128]{3,0,2,1:T(8,128)S(1)} %bitcast.3) | data formatting | bytes 65536
Async XLA Ops:
  56.9 1.3 %copy-start = (f32[2,2,16,128]{3,2,1,0:T(8,128)S(1)}, f32[2,2,16,128]{3,2,1,0:T(8,128)}, u32[]{:S(2)}) copy-start(f32[2,2,16,128]{3,2,1,0:T(8,128)} %get-tuple-element.5) | copy-start | bytes 98308

commit v2 on v1

v2 whole, which is shorter than its diff:
```python
import functools
import math

import jax
import jax.numpy as jnp
from jax import lax
from jax.experimental import pallas as pl
from jax.experimental.pallas import tpu as pltpu
from jax.sharding import PartitionSpec as P

MESH = pl.DeviceIdType.MESH
F32 = jnp.float32
BF16 = jnp.bfloat16

RADIAL = 8
SPECIES = 4
HEADS = 16
N = 128
CH = 256
CUT = 6.0
SOFT = 0.01
SPACE = CUT / (RADIAL - 1)
COEF = [math.exp(8.0 * k - k * k) for k in range(RADIAL)]
DIRS = [(dx, dy) for dx in (-1, 0, 1) for dy in (-1, 0, 1) if (dx, dy) != (0, 0)]
OWN = 4 * N
HALO = 5 * N
ROWS = 32
BLOCKS = N // ROWS


def nn(a, b):
    return lax.dot_general(a, b, (((1,), (0,)), ((), ())), preferred_element_type=F32)


def tn(a, b):
    return lax.dot_general(a, b, (((0,), (0,)), ((), ())), preferred_element_type=F32)


def nt(a, b):
    return lax.dot_general(a, b, (((1,), (1,)), ((), ())), preferred_element_type=F32)


def border(d):
    return {1: 2, -1: 1, 0: pl.ds(1, 2)}[d]


def landing(d):
    return {1: 0, -1: 3, 0: pl.ds(1, 2)}[d]


def beyond(d):
    return {1: 3, -1: 0, 0: pl.ds(1, 2)}[d]


def own_slot(c):
    return 1 + c // 2, 1 + c % 2


def halo_slots(c):
    a_out, b_out = 3 * (c // 2), 3 * (c % 2)
    return [(a_out, b_out), (a_out, 1), (a_out, 2), (1, b_out), (2, b_out)]


def loop(steps, body):
    lax.fori_loop(0, steps, body, 0)


def sigmoid(x):
    return 1.0 / (1.0 + jnp.exp(-x))


def kernel(
    nx, ny,
    pos_ref, valid_ref, spec_ref, table_ref, gain_ref, readout_ref,
    forces_ref, energies_ref,
    atoms, xi, basis_0, basis_1, basis_2, basis_3, u_s, a_s, rc_s, ri_s, dens, hid, hid_own, slope,
    msg, gms, tab_t, tab_s, gk, read_t, second, back_t, gm_own, gm_b,
    gpart, grecv, gsum, fi, fj, fpart, frecv, gs_a, gs_b,
    send_sem, recv_sem,
):
    gx, gy = lax.axis_index("gx"), lax.axis_index("gy")
    basis = (basis_0, basis_1, basis_2, basis_3)
    own_slots = [own_slot(c) for c in range(4)]

    def there(dx, dy):
        ok = None
        for d, g, n in ((dx, gx, nx), (dy, gy, ny)):
            if d:
                one = (g < n - 1) if d > 0 else (g > 0)
                ok = one if ok is None else jnp.logical_and(ok, one)
        return ok

    def copy(r, n, src, dst, peer):
        return pltpu.make_async_remote_copy(
            src_ref=src, dst_ref=dst, send_sem=send_sem.at[r, n], recv_sem=recv_sem.at[r, n],
            device_id=peer, device_id_type=MESH,
        )

    def outward(r, buf, wait):
        for n, (dx, dy) in enumerate(DIRS):
            src = buf.at[border(dx), border(dy)]
            dst = buf.at[landing(dx), landing(dy)]
            if wait == "recv":
                @pl.when(there(-dx, -dy))
                def _():
                    copy(r, n, src, dst, (gx - dx, gy - dy)).wait_recv()
            else:
                @pl.when(there(dx, dy))
                def _():
                    c = copy(r, n, src, dst, (gx + dx, gy + dy))
                    c.start() if wait == "start" else c.wait_send()

    def inward(r, buf, land, wait):
        for n, (dx, dy) in enumerate(DIRS):
            src = buf.at[beyond(dx), beyond(dy)]
            dst = land.at[n, 0] if dx and dy else land.at[n]
            if wait == "recv":
                @pl.when(there(-dx, -dy))
                def _():
                    copy(r, n, src, dst, (gx - dx, gy - dy)).wait_recv()
            else:
                @pl.when(there(dx, dy))
                def _():
                    c = copy(r, n, src, dst, (gx + dx, gy + dy))
                    c.start() if wait == "start" else c.wait_send()

    def returned(land, a, b):
        total = None
        for n, (dx, dy) in enumerate(DIRS):
            if (dx == 0 or a == (1 if dx == 1 else 2)) and (dy == 0 or b == (1 if dy == 1 else 2)):
                m = a - 1 if dx == 0 else (b - 1 if dy == 0 else 0)
                total = land[n, m] if total is None else total + land[n, m]
        return total

    for a in range(4):
        for b in range(4):
            if a in (1, 2) and b in (1, 2):
                rows = [pos_ref[i, a - 1, b - 1 : b, :] for i in range(3)]
                rows.append(valid_ref[a - 1, b - 1 : b, :].astype(F32))
                rows.append(spec_ref[a - 1, b - 1 : b, :].astype(F32))
                rows.append(jnp.zeros((3, N), F32))
                atoms[a, b] = jnp.concatenate(rows, 0)
            else:
                atoms[a, b] = jnp.zeros((8, N), F32)
                dens[a, b] = jnp.zeros((RADIAL * SPECIES, N), F32)
    grecv[...] = jnp.zeros_like(grecv)
    frecv[...] = jnp.zeros_like(frecv)

    barrier = pltpu.get_barrier_semaphore()
    for dx, dy in DIRS:
        @pl.when(there(dx, dy))
        def _():
            pl.semaphore_signal(barrier, inc=1, device_id=(gx + dx, gy + dy), device_id_type=MESH)
    span_x = 1 + jnp.where(gx > 0, 1, 0) + jnp.where(gx < nx - 1, 1, 0)
    span_y = 1 + jnp.where(gy > 0, 1, 0) + jnp.where(gy < ny - 1, 1, 0)

    table = table_ref[...] * 0.125
    high = table.astype(BF16).astype(F32)
    low = table - high
    tab_s[...] = jnp.concatenate([high, low], 0).astype(BF16)
    stacked = jnp.concatenate([high, high, low, jnp.zeros((32, CH), F32)], 0)
    tab_t[...] = stacked.astype(BF16)
    for k in range(RADIAL):
        row = gain_ref[k : k + 1, :] * (COEF[k] / 32.0)
        gk[k] = row
    read_t[...] = jnp.concatenate([readout_ref[...], jnp.zeros((N - HEADS, CH), BF16)], 0)
    for c in range(4):
        a, b = own_slot(c)
        tile = atoms[a, b]
        x = jnp.where(tile[3:4] > 0.0, tile[0:1], 1e4)
        xi[c, 0] = jnp.broadcast_to(x, (N, N)).T
        xi[c, 1] = jnp.broadcast_to(tile[1:2], (N, N)).T
        xi[c, 2] = jnp.broadcast_to(tile[2:3], (N, N)).T

    pl.semaphore_wait(barrier, span_x * span_y - 1)
    outward(0, atoms, "start")

    def offsets(c, rows, a, b):
        xj = jnp.where(atoms[a, b, 3:4, :] > 0.0, atoms[a, b, 0:1, :], -1e4)
        dx = xi[c, 0, rows, :] - xj
        dy = xi[c, 1, rows, :] - atoms[a, b, 1:2, :]
        dz = xi[c, 2, rows, :] - atoms[a, b, 2:3, :]
        return dx, dy, dz

    def pair_basis(c, block, a, b, lane, self_cell):
        rows = slice(block * ROWS, (block + 1) * ROWS)
        cols = slice(lane, lane + N)
        dx, dy, dz = offsets(c, rows, a, b)
        sq = dx * dx + dy * dy + (dz * dz + SOFT)
        if self_cell:
            i = lax.broadcasted_iota(jnp.int32, (ROWS, N), 0) + block * ROWS
            j = lax.broadcasted_iota(jnp.int32, (ROWS, N), 1)
            sq = jnp.where(i == j, 1e8, sq)
        ri = lax.rsqrt(sq)
        reach = jnp.maximum(1.0 - sq * (1.0 / (CUT * CUT)), 0.0)
        t = jnp.minimum(sq * ri * (1.0 / SPACE), float(RADIAL - 1))
        u = jnp.exp(2.0 * t - 8.0)
        amp = jnp.exp(-(t * t)) * reach
        u_s[c, rows, cols] = u
        a_s[c, rows, cols] = amp
        rc_s[c, rows, cols] = reach
        ri_s[c, rows, cols] = ri
        term = amp * reach
        for k in range(RADIAL):
            basis[c][k * N + block * ROWS : k * N + (block + 1) * ROWS, cols] = term.astype(BF16)
            if k < RADIAL - 1:
                term = term * u

    def own_pairs(c):
        for block in range(BLOCKS):
            for j, (a, b) in enumerate(own_slots):
                pair_basis(c, block, a, b, j * N, c == j)

    def halo_pairs(c):
        for block in range(BLOCKS):
            for m, (a, b) in enumerate(halo_slots(c)):
                pair_basis(c, block, a, b, OWN + m * N, False)

    def kinds(a, b, rows):
        kind = atoms[a, b, 4:5, :].astype(jnp.int32)
        r = lax.broadcasted_iota(jnp.int32, (rows, N), 0)
        return r, kind

    def selector(a, b):
        r, kind = kinds(a, b, N)
        hit = jnp.logical_and(r < 64, (r & 3) == kind)
        hid[a, b, :, CH:] = jnp.where(hit, 1.0, 0.0).T.astype(BF16)

    def hot(slots):
        parts = []
        for a, b in slots:
            r, kind = kinds(a, b, 16)
            parts.append(jnp.where(r == kind, 1.0, 0.0).astype(BF16))
        return jnp.concatenate(parts, 1)

    def own_density(c):
        out = nt(hot(own_slots), basis[c][:, 0:OWN])
        a, b = own_slots[c]
        for k in range(RADIAL):
            dens[a, b, k * SPECIES : (k + 1) * SPECIES, :] = (
                out[0:SPECIES, k * N : (k + 1) * N] * COEF[k]
            )

    def halo_density(c):
        out = nt(hot(halo_slots(c)), basis[c][:, OWN:])
        a, b = own_slots[c]
        for k in range(RADIAL):
            dens[a, b, k * SPECIES : (k + 1) * SPECIES, :] += (
                out[0:SPECIES, k * N : (k + 1) * N] * COEF[k]
            )

    own_pairs(0)
    for c in range(1, 4):
        own_pairs(c)
        own_density(c - 1)
    for a, b in own_slots:
        selector(a, b)
    outward(0, atoms, "recv")
    for c in range(4):
        for m in range(3):
            selector(*[(0, m), (3, m + 1), (m + 1, 0), (m, 3)][c])
        halo_pairs(c)
        halo_density(c - 1) if c else own_density(3)
    halo_density(3)
    outward(1, dens, "start")

    def features(slots):
        parts = []
        for a, b in slots:
            d = dens[a, b]
            top = d.astype(BF16)
            rest = (d - top.astype(F32)).astype(BF16)
            parts.append(jnp.concatenate([top, rest, top, jnp.zeros((32, N), BF16)], 0))
        z = tn(jnp.concatenate(parts, 1), tab_t[...])
        s = sigmoid(z)
        h = z * s
        sp = s * (1.0 + z * (1.0 - s))
        for m, (a, b) in enumerate(slots):
            rows = slice(m * N, (m + 1) * N)
            hid[a, b, :, 0:CH] = h[rows].astype(BF16)
            slope[a, b] = sp[rows]
        return h

    h = features(own_slots)
    for c in range(4):
        hid_own[c] = h[c * N : (c + 1) * N]

    def gained(prod):
        total = prod[0:N] * gk[0]
        for k in range(1, RADIAL):
            total = total + prod[k * N : (k + 1) * N] * gk[k]
        return total

    h = jnp.concatenate([hid[a, b, :, 0:CH] for a, b in own_slots], 0)
    for c in range(4):
        msg[c] = gained(nn(basis[c][:, 0:OWN], h))
    outward(1, dens, "recv")

    features([(0, b) for b in range(4)])
    features([(3, b) for b in range(4)])
    features([(1, 0), (2, 0), (1, 3), (2, 3)])

    for c in range(4):
        h = jnp.concatenate([hid[a, b, :, 0:CH] for a, b in halo_slots(c)], 0)
        p = msg[c] + gained(nn(basis[c][:, OWN:], h)) + hid_own[c]
        s = sigmoid(p)
        second[c * N : (c + 1) * N, :] = (p * s).astype(BF16)
        msg[c] = s * (1.0 + p * (1.0 - s))

    heads = nt(read_t[0:HEADS, :], second[...])
    sh = sigmoid(heads)
    valid = jnp.concatenate([atoms[a, b, 3:4, :] for a, b in own_slots], 1)
    out = valid * (heads * sh)
    back = (valid * (1.0 / HEADS)) * (sh * (1.0 + heads * (1.0 - sh)))
    for c, (a, b) in enumerate(own_slots):
        cols = slice(c * N, (c + 1) * N)
        for h in range(HEADS):
            energies_ref[h, a - 1, b - 1 : b, :] = out[h : h + 1, cols]
        tile = jnp.concatenate([back[:, cols], jnp.zeros((N - HEADS, N), F32)], 0)
        back_t[c] = tile.T.astype(BF16)

    def project(x):
        out = nt(tab_s[...], x)
        return out[0:32] + out[32:64]

    def head_grad(c):
        dsec = nn(back_t[c], read_t[...]).astype(BF16).astype(F32)
        gm = dsec * msg[c]
        gm_own[c] = gm
        gm_b[c * N : (c + 1) * N, :] = gm.astype(BF16)
        for k in range(RADIAL):
            gms[c, k * N : (k + 1) * N, 0:CH] = (gm * gk[k]).astype(BF16)

    def halo_grad(c):
        x = tn(basis[c][:, OWN:], gms[c, :, 0:CH])
        slots = halo_slots(c)
        x = x * jnp.concatenate([slope[a, b] for a, b in slots], 0)
        out = project(x.astype(BF16))
        for m, (a, b) in enumerate(slots):
            gpart[a, b] += out[:, m * N : (m + 1) * N]

    gpart[...] = jnp.zeros_like(gpart)
    head_grad(0)
    for c in range(4):
        if c < 3:
            head_grad(c + 1)
        halo_grad(c)
    inward(2, gpart, grecv, "start")

    for c, (a, b) in enumerate(own_slots):
        x = gained(nn(basis[c][:, 0:OWN], gm_b[...])) + gm_own[c]
        gsum[c] = project((x * slope[a, b]).astype(BF16))
    inward(2, gpart, grecv, "recv")

    for c in range(4):
        a, b = own_slot(c)
        g = gsum[c] + returned(grecv, a, b)
        r = lax.broadcasted_iota(jnp.int32, (32, N), 0) >> 2
        coef = jnp.full((32, N), COEF[0], F32)
        for k in range(1, RADIAL):
            coef = jnp.where(r == k, COEF[k], coef)
        g = g * coef
        top = g.astype(BF16).astype(F32)
        gt = jnp.concatenate([top, g - top, jnp.zeros((64, N), F32)], 0).T
        lane = lax.broadcasted_iota(jnp.int32, (N, N), 1)
        for k in range(RADIAL):
            keep = jnp.logical_and(lane < 64, ((lane & 31) >> 2) == k)
            gms[c, k * N : (k + 1) * N, CH:] = jnp.where(keep, gt, 0.0).astype(BF16)

    fj[...] = jnp.zeros_like(fj)

    def gradients(step, buf):
        c = step % 4
        slots = halo_slots(c) if step < 4 else own_slots
        h = jnp.concatenate([hid[a, b] for a, b in slots], 0)
        buf[:, 0 : h.shape[0]] = nt(gms[c], h)

    def block_forces(c, block, slots, lane0, buf):
        rows = slice(block * ROWS, (block + 1) * ROWS)
        sums = [jnp.zeros((ROWS, N), F32) for _ in range(3)]
        for m, (a, b) in enumerate(slots):
            cols = slice(lane0 + m * N, lane0 + (m + 1) * N)
            u = u_s[c, rows, cols]

            def grad(k):
                return buf[k * N + block * ROWS : k * N + (block + 1) * ROWS, m * N : (m + 1) * N]

            poly = grad(RADIAL - 1)
            slant = poly
            for k in range(RADIAL - 2, -1, -1):
                poly = poly * u + grad(k)
                if k:
                    slant = slant * u + poly
            slant = slant * u
            reach = rc_s[c, rows, cols]
            inner = ri_s[c, rows, cols] * slant * (2.0 / SPACE) - poly * (2.0 / SPACE**2)
            force = a_s[c, rows, cols] * (reach * inner - poly * (4.0 / CUT**2))
            for i, d in enumerate(offsets(c, rows, a, b)):
                f = force * d
                sums[i] = sums[i] + f
                part = f[0:8]
                for q in range(1, ROWS // 8):
                    part = part + f[8 * q : 8 * q + 8]
                fj[a, b, i] += part
        for i in range(3):
            if lane0:
                fi[c, i, rows, :] = sums[i]
            else:
                fi[c, i, rows, :] += sums[i]

    def pair_forces(step, buf):
        c = step % 4
        slots, lane0 = (halo_slots(c), OWN) if step < 4 else (own_slots, 0)
        for block in range(BLOCKS):
            block_forces(c, block, slots, lane0, buf)

    bufs = (gs_a, gs_b)
    gradients(0, gs_a)
    for step in range(4):
        pair_forces(step, bufs[step % 2])
        gradients(step + 1, bufs[(step + 1) % 2])
    for a in range(4):
        for b in range(4):
            if not (a in (1, 2) and b in (1, 2)):
                rows = [jnp.sum(fj[a, b, i], 0, keepdims=True) for i in range(3)]
                fpart[a, b] = jnp.concatenate(rows + [jnp.zeros((5, N), F32)], 0)
    inward(3, fpart, frecv, "start")
    for step in range(4, 8):
        pair_forces(step, bufs[step % 2])
        if step < 7:
            gradients(step + 1, bufs[(step + 1) % 2])
    sums = []
    for c in range(4):
        a, b = own_slot(c)
        rows = []
        for i in range(3):
            mine = jnp.sum(fi[c, i].T, 0, keepdims=True)
            rows.append(jnp.sum(fj[a, b, i], 0, keepdims=True) - mine)
        sums.append(jnp.concatenate(rows + [jnp.zeros((5, N), F32)], 0))
    inward(3, fpart, frecv, "recv")
    for c in range(4):
        a, b = own_slot(c)
        total = sums[c] + returned(frecv, a, b)
        for i in range(3):
            forces_ref[i, a - 1, b - 1 : b, :] = total[i : i + 1]
    outward(0, atoms, "send")
    outward(1, dens, "send")
    inward(2, gpart, grecv, "send")
    inward(3, fpart, frecv, "send")


def shards(nx, ny, positions, valid_mask, species, density_table, radial_gain, readout):
    vmem = pltpu.VMEM
    whole = pl.BlockSpec(memory_space=pltpu.VMEM)
    wide = OWN + HALO
    forces, energies = pl.pallas_call(
        functools.partial(kernel, nx, ny),
        out_shape=(
            jax.ShapeDtypeStruct((3, 2, 2, N), F32),
            jax.ShapeDtypeStruct((HEADS, 2, 2, N), F32),
        ),
        in_specs=[whole] * 6,
        out_specs=(whole, whole),
        scratch_shapes=[
            vmem((4, 4, 8, N), F32),
            vmem((4, 3, N, N), F32),
            vmem((RADIAL * N, wide), BF16),
            vmem((RADIAL * N, wide), BF16),
            vmem((RADIAL * N, wide), BF16),
            vmem((RADIAL * N, wide), BF16),
            vmem((4, N, wide), F32),
            vmem((4, N, wide), F32),
            vmem((4, N, wide), F32),
            vmem((4, N, wide), F32),
            vmem((4, 4, RADIAL * SPECIES, N), F32),
            vmem((4, 4, N, CH + N), BF16),
            vmem((4, N, CH), F32),
            vmem((4, 4, N, CH), F32),
            vmem((4, N, CH), F32),
            vmem((4, RADIAL * N, CH + N), BF16),
            vmem((N, CH), BF16),
            vmem((64, CH), BF16),
            vmem((RADIAL, 1, CH), F32),
            vmem((N, CH), BF16),
            vmem((OWN, CH), BF16),
            vmem((4, N, N), BF16),
            vmem((4, N, CH), F32),
            vmem((OWN, CH), BF16),
            vmem((4, 4, 32, N), F32),
            vmem((8, 2, 32, N), F32),
            vmem((4, 32, N), F32),
            vmem((4, 3, N, N), F32),
            vmem((4, 4, 3, 8, N), F32),
            vmem((4, 4, 8, N), F32),
            vmem((8, 2, 8, N), F32),
            vmem((RADIAL * N, HALO), F32),
            vmem((RADIAL * N, HALO), F32),
            pltpu.SemaphoreType.DMA((4, 8)),
            pltpu.SemaphoreType.DMA((4, 8)),
        ],
        compiler_params=pltpu.CompilerParams(
            collective_id=0, has_side_effects=True, vmem_limit_bytes=56 * 1024 * 1024
        ),
    )(positions, valid_mask, species, density_table, radial_gain, readout.T)
    return forces, energies


def solution(mesh):
    nx, ny = mesh.shape["gx"], mesh.shape["gy"]
    in_specs = (P(None, "gx", "gy", None), P("gx", "gy", None), P("gx", "gy", None), P(), P(), P())
    out_specs = (P(None, "gx", "gy", None), P(None, "gx", "gy", None))
    return jax.shard_map(
        functools.partial(shards, nx, ny), mesh=mesh, in_specs=in_specs, out_specs=out_specs,
        check_vma=False,
    )
```

time: 59.1 us -> 49.2 us (0.83)
  Pallas kernels: 54.8 us -> 45.6 us
  local copies, waits for them, and re-layouts: 3.37 us -> 2.66 us
    pallas_call x1, Pallas kernels: 54.8 us -> 45.6 us  [shards(): pl.pallas_call(functools.partial(kernel, nx, ny), out_shape=(jax.ShapeDty...]
    transpose x1 -> x0, local copies, waits for them, and re-layouts: 0.73 us -> none  [shards(): forces[:, :, :3].transpose(2, 0, 1, 3)]
    unnamed x5 -> x2, local copies, waits for them, and re-layouts: 2.65 us -> 2.66 us
where the time goes in v2:
time: 49.2 us; the launch traced here: 48.9 us
  Pallas kernels  45.6 us (93%)
  local copies, waits for them, and re-layouts  2.66 us (5%)
  between operations  0.64 us (1%)
    pallas_call x1, Pallas kernels, shards(): pl.pallas_call(functools.partial(kernel, nx, ny), out_shape=(jax.ShapeDty...  45.6 us
    unnamed x2, local copies, waits for them, and re-layouts  2.66 us

profile of v2, /device:TPU:95, one launch (start us, length us, event | category | flops | bytes accessed | tf_op | source)
XLA Modules:
  0.0 48.9 jit_solution(6122340292743026726)
XLA Ops:
  0.6 45.6 %shard_map.77 = (f32[3,2,2,128]{3,2,1,0:T(2,128)}, f32[16,2,2,128]{3,2,1,0:T(2,128)}) custom-call(f32[3,2,2,128]{3,2,1,0:T(2,128)} %pos_ref.1, s32[2,2,128]{2,1,0:T(2,128)} %valid_ref.1, s32[2,2,128]{2,1,0:T(2,128)} %spec_ref.1, f32[32,256]{1,0:T(8,128)} %table_ref.1, f32[8,256]{1,0:T(8,128)} %gain_ref.1, bf16[16,256]{1,0:T(8,128)(2,1)} %bitcast.1), custom_call_target="tpu_custom_call" | custom-call | tf_op jit(solution)/shard_map/pallas_call | solution.py:456
  46.2 1.3 %copy.10 = f32[3,2,2,128]{3,2,1,0:T(2,128)} copy(f32[3,2,2,128]{3,2,1,0:T(2,128)} %get-tuple-element.4) | data formatting | bytes 12288
  47.5 1.4 %copy.11 = f32[16,2,2,128]{3,2,1,0:T(2,128)} copy(f32[16,2,2,128]{3,2,1,0:T(2,128)} %get-tuple-element.5) | data formatting | bytes 65536

commit v3 on v2

--- a/solution.py
+++ b/solution.py
@@ -21,7 +21,8 @@
 SOFT = 0.01
 SPACE = CUT / (RADIAL - 1)
 COEF = [math.exp(8.0 * k - k * k) for k in range(RADIAL)]
-DIRS = [(dx, dy) for dx in (-1, 0, 1) for dy in (-1, 0, 1) if (dx, dy) != (0, 0)]
+DIRS = [(-1, -1), (-1, 1), (1, -1), (1, 1), (-1, 0), (1, 0), (0, -1), (0, 1)]
+CORNERS, XSIDES, YSIDES = (0, 1, 2, 3), (4, 5), (6, 7)
 OWN = 4 * N
 HALO = 5 * N
 ROWS = 32
@@ -56,13 +57,32 @@
     return 1 + c // 2, 1 + c % 2
 
 
+def y_slots(c):
+    return [(1, 3 * (c % 2)), (2, 3 * (c % 2))]
+
+
+def x_slots(c):
+    return [(3 * (c // 2), 1), (3 * (c // 2), 2)]
+
+
+def corner_slots(c):
+    return [(3 * (c // 2), 3 * (c % 2))]
+
+
 def halo_slots(c):
-    a_out, b_out = 3 * (c // 2), 3 * (c % 2)
-    return [(a_out, b_out), (a_out, 1), (a_out, 2), (1, b_out), (2, b_out)]
-
-
-def loop(steps, body):
-    lax.fori_loop(0, steps, body, 0)
+    return y_slots(c) + x_slots(c) + corner_slots(c)
+
+
+COMPLETE = ((0,), (1, 4), (2, 6), (3, 5, 7))
+NEEDED = ((3, 5, 7), (2, 6), (1, 4), (0,))
+
+
+PARTS = (
+    (lambda c: [own_slot(j) for j in range(4)], 0, ()),
+    (y_slots, OWN, YSIDES),
+    (x_slots, OWN + 2 * N, XSIDES),
+    (corner_slots, OWN + 4 * N, CORNERS),
+)
 
 
 def sigmoid(x):
@@ -71,15 +91,25 @@
 
 def kernel(
     nx, ny,
-    pos_ref, valid_ref, spec_ref, table_ref, gain_ref, readout_ref,
+    pos_hbm, valid_hbm, spec_hbm, table_hbm, gain_hbm, readout_hbm,
     forces_ref, energies_ref,
     atoms, xi, basis_0, basis_1, basis_2, basis_3, u_s, a_s, rc_s, ri_s, dens, hid, hid_own, slope,
     msg, gms, tab_t, tab_s, gk, read_t, second, back_t, gm_own, gm_b,
     gpart, grecv, gsum, fi, fj, fpart, frecv, gs_a, gs_b,
+    pos_ref, valid_ref, spec_ref, table_ref, gain_ref, readout_ref, load_sem,
     send_sem, recv_sem,
 ):
     gx, gy = lax.axis_index("gx"), lax.axis_index("gy")
     basis = (basis_0, basis_1, basis_2, basis_3)
+    loads = [
+        pltpu.make_async_copy(src, dst, load_sem.at[i])
+        for i, (src, dst) in enumerate((
+            (pos_hbm, pos_ref), (valid_hbm, valid_ref), (spec_hbm, spec_ref),
+            (table_hbm, table_ref), (gain_hbm, gain_ref), (readout_hbm, readout_ref),
+        ))
+    ]
+    for load in loads:
+        load.start()
     own_slots = [own_slot(c) for c in range(4)]
 
     def there(dx, dy):
@@ -96,8 +126,9 @@
             device_id=peer, device_id_type=MESH,
         )
 
-    def outward(r, buf, wait):
-        for n, (dx, dy) in enumerate(DIRS):
+    def outward(r, buf, wait, dirs=range(8)):
+        for n in dirs:
+            dx, dy = DIRS[n]
             src = buf.at[border(dx), border(dy)]
             dst = buf.at[landing(dx), landing(dy)]
             if wait == "recv":
@@ -110,8 +141,9 @@
                     c = copy(r, n, src, dst, (gx + dx, gy + dy))
                     c.start() if wait == "start" else c.wait_send()
 
-    def inward(r, buf, land, wait):
-        for n, (dx, dy) in enumerate(DIRS):
+    def inward(r, buf, land, wait, dirs=range(8)):
+        for n in dirs:
+            dx, dy = DIRS[n]
             src = buf.at[beyond(dx), beyond(dy)]
             dst = land.at[n, 0] if dx and dy else land.at[n]
             if wait == "recv":
@@ -134,13 +166,7 @@
 
     for a in range(4):
         for b in range(4):
-            if a in (1, 2) and b in (1, 2):
-                rows = [pos_ref[i, a - 1, b - 1 : b, :] for i in range(3)]
-                rows.append(valid_ref[a - 1, b - 1 : b, :].astype(F32))
-                rows.append(spec_ref[a - 1, b - 1 : b, :].astype(F32))
-                rows.append(jnp.zeros((3, N), F32))
-                atoms[a, b] = jnp.concatenate(rows, 0)
-            else:
+            if not (a in (1, 2) and b in (1, 2)):
                 atoms[a, b] = jnp.zeros((8, N), F32)
                 dens[a, b] = jnp.zeros((RADIAL * SPECIES, N), F32)
     grecv[...] = jnp.zeros_like(grecv)
@@ -153,6 +179,15 @@
             pl.semaphore_signal(barrier, inc=1, device_id=(gx + dx, gy + dy), device_id_type=MESH)
     span_x = 1 + jnp.where(gx > 0, 1, 0) + jnp.where(gx < nx - 1, 1, 0)
     span_y = 1 + jnp.where(gy > 0, 1, 0) + jnp.where(gy < ny - 1, 1, 0)
+
+    for load in loads:
+        load.wait()
+    for a, b in own_slots:
+        rows = [pos_ref[i, a - 1, b - 1 : b, :] for i in range(3)]
+        rows.append(valid_ref[a - 1, b - 1 : b, :].astype(F32))
+        rows.append(spec_ref[a - 1, b - 1 : b, :].astype(F32))
+        rows.append(jnp.zeros((3, N), F32))
+        atoms[a, b] = jnp.concatenate(rows, 0)
 
     table = table_ref[...] * 0.125
     high = table.astype(BF16).astype(F32)
@@ -206,15 +241,11 @@
             if k < RADIAL - 1:
                 term = term * u
 
-    def own_pairs(c):
+    def part_pairs(c, part):
+        slots_of, lane0, _ = PARTS[part]
         for block in range(BLOCKS):
-            for j, (a, b) in enumerate(own_slots):
-                pair_basis(c, block, a, b, j * N, c == j)
-
-    def halo_pairs(c):
-        for block in range(BLOCKS):
-            for m, (a, b) in enumerate(halo_slots(c)):
-                pair_basis(c, block, a, b, OWN + m * N, False)
+            for m, (a, b) in enumerate(slots_of(c)):
+                pair_basis(c, block, a, b, lane0 + m * N, part == 0 and m == c)
 
     def kinds(a, b, rows):
         kind = atoms[a, b, 4:5, :].astype(jnp.int32)
@@ -233,35 +264,29 @@
             parts.append(jnp.where(r == kind, 1.0, 0.0).astype(BF16))
         return jnp.concatenate(parts, 1)
 
-    def own_density(c):
-        out = nt(hot(own_slots), basis[c][:, 0:OWN])
+    def part_density(c, part):
+        slots_of, lane0, _ = PARTS[part]
+        slots = slots_of(c)
+        out = nt(hot(slots), basis[c][:, lane0 : lane0 + len(slots) * N])
         a, b = own_slots[c]
         for k in range(RADIAL):
-            dens[a, b, k * SPECIES : (k + 1) * SPECIES, :] = (
-                out[0:SPECIES, k * N : (k + 1) * N] * COEF[k]
-            )
-
-    def halo_density(c):
-        out = nt(hot(halo_slots(c)), basis[c][:, OWN:])
-        a, b = own_slots[c]
-        for k in range(RADIAL):
-            dens[a, b, k * SPECIES : (k + 1) * SPECIES, :] += (
-                out[0:SPECIES, k * N : (k + 1) * N] * COEF[k]
-            )
-
-    own_pairs(0)
-    for c in range(1, 4):
-        own_pairs(c)
-        own_density(c - 1)
-    for a, b in own_slots:
-        selector(a, b)
-    outward(0, atoms, "recv")
-    for c in range(4):
-        for m in range(3):
-            selector(*[(0, m), (3, m + 1), (m + 1, 0), (m, 3)][c])
-        halo_pairs(c)
-        halo_density(c - 1) if c else own_density(3)
-    halo_density(3)
+            rows = slice(k * SPECIES, (k + 1) * SPECIES)
+            piece = out[0:SPECIES, k * N : (k + 1) * N] * COEF[k]
+            dens[a, b, rows, :] = dens[a, b, rows, :] + piece if part else piece
+
+    last = None
+    for part in range(4):
+        if part:
+            outward(0, atoms, "recv", PARTS[part][2])
+        slots_of = PARTS[part][0]
+        for a, b in sorted({slot for c in range(4) for slot in slots_of(c)}):
+            selector(a, b)
+        for c in range(4):
+            part_pairs(c, part)
+            if last:
+                part_density(*last)
+            last = (c, part)
+    part_density(*last)
     outward(1, dens, "start")
 
     def features(slots):
@@ -291,18 +316,23 @@
             total = total + prod[k * N : (k + 1) * N] * gk[k]
         return total
 
-    h = jnp.concatenate([hid[a, b, :, 0:CH] for a, b in own_slots], 0)
-    for c in range(4):
-        msg[c] = gained(nn(basis[c][:, 0:OWN], h))
-    outward(1, dens, "recv")
-
-    features([(0, b) for b in range(4)])
-    features([(3, b) for b in range(4)])
-    features([(1, 0), (2, 0), (1, 3), (2, 3)])
-
-    for c in range(4):
-        h = jnp.concatenate([hid[a, b, :, 0:CH] for a, b in halo_slots(c)], 0)
-        p = msg[c] + gained(nn(basis[c][:, OWN:], h)) + hid_own[c]
+    def part_message(c, part):
+        slots_of, lane0, _ = PARTS[part]
+        slots = slots_of(c)
+        h = jnp.concatenate([hid[a, b, :, 0:CH] for a, b in slots], 0)
+        return gained(nn(basis[c][:, lane0 : lane0 + len(slots) * N], h))
+
+    for c in range(4):
+        msg[c] = part_message(c, 0) + hid_own[c]
+    for part in (1, 2):
+        outward(1, dens, "recv", PARTS[part][2])
+        features(sorted({slot for c in range(4) for slot in PARTS[part][0](c)}))
+        for c in range(4):
+            msg[c] += part_message(c, part)
+    outward(1, dens, "recv", CORNERS)
+    features([corner_slots(c)[0] for c in range(4)])
+    for c in range(4):
+        p = msg[c] + part_message(c, 3)
         s = sigmoid(p)
         second[c * N : (c + 1) * N, :] = (p * s).astype(BF16)
         msg[c] = s * (1.0 + p * (1.0 - s))
@@ -345,14 +375,13 @@
         if c < 3:
             head_grad(c + 1)
         halo_grad(c)
-    inward(2, gpart, grecv, "start")
+        inward(2, gpart, grecv, "start", COMPLETE[c])
 
     for c, (a, b) in enumerate(own_slots):
         x = gained(nn(basis[c][:, 0:OWN], gm_b[...])) + gm_own[c]
         gsum[c] = project((x * slope[a, b]).astype(BF16))
-    inward(2, gpart, grecv, "recv")
-
-    for c in range(4):
+    def density_grad(c):
+        inward(2, gpart, grecv, "recv", NEEDED[c])
         a, b = own_slot(c)
         g = gsum[c] + returned(grecv, a, b)
         r = lax.broadcasted_iota(jnp.int32, (32, N), 0) >> 2
@@ -414,17 +443,24 @@
         for block in range(BLOCKS):
             block_forces(c, block, slots, lane0, buf)
 
+    def halo_force(n):
+        dx, dy = DIRS[n]
+        for a in {1: (3,), -1: (0,), 0: (1, 2)}[dx]:
+            for b in {1: (3,), -1: (0,), 0: (1, 2)}[dy]:
+                rows = [jnp.sum(fj[a, b, i], 0, keepdims=True) for i in range(3)]
+                fpart[a, b] = jnp.concatenate(rows + [jnp.zeros((5, N), F32)], 0)
+
     bufs = (gs_a, gs_b)
+    density_grad(0)
     gradients(0, gs_a)
     for step in range(4):
+        if step < 3:
+            density_grad(step + 1)
         pair_forces(step, bufs[step % 2])
         gradients(step + 1, bufs[(step + 1) % 2])
-    for a in range(4):
-        for b in range(4):
-            if not (a in (1, 2) and b in (1, 2)):
-                rows = [jnp.sum(fj[a, b, i], 0, keepdims=True) for i in range(3)]
-                fpart[a, b] = jnp.concatenate(rows + [jnp.zeros((5, N), F32)], 0)
-    inward(3, fpart, frecv, "start")
+        for n in COMPLETE[step]:
+            halo_force(n)
+        inward(3, fpart, frecv, "start", COMPLETE[step])
     for step in range(4, 8):
         pair_forces(step, bufs[step % 2])
         if step < 7:
@@ -449,6 +485,11 @@
     inward(3, fpart, frecv, "send")
 
 
+def hand_over(forces_ref, energies_ref, forces_out, energies_out):
+    forces_out[...] = forces_ref[...]
+    energies_out[...] = energies_ref[...]
+
+
 def shards(nx, ny, positions, valid_mask, species, density_table, radial_gain, readout):
     vmem = pltpu.VMEM
     whole = pl.BlockSpec(memory_space=pltpu.VMEM)
@@ -456,10 +497,10 @@
     forces, energies = pl.pallas_call(
         functools.partial(kernel, nx, ny),
         out_shape=(
-            jax.ShapeDtypeStruct((3, 2, 2, N), F32),
-            jax.ShapeDtypeStruct((HEADS, 2, 2, N), F32),
+            pltpu.VMEM((3, 2, 2, N), F32),
+            pltpu.VMEM((HEADS, 2, 2, N), F32),
         ),
-        in_specs=[whole] * 6,
+        in_specs=[pl.BlockSpec(memory_space=pl.ANY)] * 6,
         out_specs=(whole, whole),
         scratch_shapes=[
             vmem((4, 4, 8, N), F32),
@@ -495,6 +536,13 @@
             vmem((8, 2, 8, N), F32),
             vmem((RADIAL * N, HALO), F32),
             vmem((RADIAL * N, HALO), F32),
+            vmem((3, 2, 2, N), F32),
+            vmem((2, 2, N), jnp.int32),
+            vmem((2, 2, N), jnp.int32),
+            vmem((RADIAL * SPECIES, CH), F32),
+            vmem((RADIAL, CH), F32),
+            vmem((HEADS, CH), BF16),
+            pltpu.SemaphoreType.DMA((6,)),
             pltpu.SemaphoreType.DMA((4, 8)),
             pltpu.SemaphoreType.DMA((4, 8)),
         ],

time: 49.2 us -> 41.8 us (0.85)
  the two profiles are of different devices: /device:TPU:95 before, /device:TPU:160 now
where the time goes in v3:
time: 41.8 us; the launch traced here: 41.7 us
  Pallas kernels  39.8 us (95%)
  local copies, waits for them, and re-layouts  1.21 us (3%)
  between operations  0.64 us (2%)
    pallas_call x1, Pallas kernels, shards(): pl.pallas_call(functools.partial(kernel, nx, ny), out_shape=(pltpu.VMEM((...  39.8 us
    unnamed x2, local copies, waits for them, and re-layouts  1.21 us

profile of v3, /device:TPU:160, one launch (start us, length us, event | category | flops | bytes accessed | tf_op | source)
XLA Modules:
  0.0 41.7 jit_solution(4214967445818671961)
XLA Ops:
  0.6 39.8 %shard_map.77 = (f32[3,2,2,128]{3,2,1,0:T(2,128)S(1)}, f32[16,2,2,128]{3,2,1,0:T(2,128)S(1)}) custom-call(f32[3,2,2,128]{3,2,1,0:T(2,128)} %pos_hbm.1, s32[2,2,128]{2,1,0:T(2,128)} %valid_hbm.1, s32[2,2,128]{2,1,0:T(2,128)} %spec_hbm.1, f32[32,256]{1,0:T(8,128)} %table_hbm.1, f32[8,256]{1,0:T(8,128)} %gain_hbm.1, bf16[16,256]{1,0:T(8,128)(2,1)} %bitcast.1), custom_call_target="tpu_custom_call" | custom-call | tf_op jit(solution)/shard_map/pallas_call | solution.py:497
  40.4 0.6 %copy.10 = f32[3,2,2,128]{3,2,1,0:T(2,128)} copy(f32[3,2,2,128]{3,2,1,0:T(2,128)S(1)} %get-tuple-element.2) | data formatting | bytes 12288
  41.0 0.6 %copy.11 = f32[16,2,2,128]{3,2,1,0:T(2,128)} copy(f32[16,2,2,128]{3,2,1,0:T(2,128)S(1)} %get-tuple-element.3) | data formatting | bytes 65536

commit v4 on v3

--- a/solution.py
+++ b/solution.py
@@ -22,7 +22,6 @@
 SPACE = CUT / (RADIAL - 1)
 COEF = [math.exp(8.0 * k - k * k) for k in range(RADIAL)]
 DIRS = [(-1, -1), (-1, 1), (1, -1), (1, 1), (-1, 0), (1, 0), (0, -1), (0, 1)]
-CORNERS, XSIDES, YSIDES = (0, 1, 2, 3), (4, 5), (6, 7)
 OWN = 4 * N
 HALO = 5 * N
 ROWS = 32
@@ -62,26 +61,23 @@
 
 
 def x_slots(c):
-    return [(3 * (c // 2), 1), (3 * (c // 2), 2)]
-
-
-def corner_slots(c):
-    return [(3 * (c // 2), 3 * (c % 2))]
+    a = 3 * (c // 2)
+    return [(a, 1), (a, 2), (a, 3 * (c % 2))]
 
 
 def halo_slots(c):
-    return y_slots(c) + x_slots(c) + corner_slots(c)
-
-
-COMPLETE = ((0,), (1, 4), (2, 6), (3, 5, 7))
-NEEDED = ((3, 5, 7), (2, 6), (1, 4), (0,))
+    return y_slots(c) + x_slots(c)
+
+
+GRAD_ORDER = ((0, (0,)), (1, (1, 4)), (2, (2, 6)), (3, (3, 5, 7)))
+NEEDED = {2: (1, 4, 7), 3: (0, 6), 0: (3, 5), 1: (2,)}
 
 
 PARTS = (
-    (lambda c: [own_slot(j) for j in range(4)], 0, ()),
-    (y_slots, OWN, YSIDES),
-    (x_slots, OWN + 2 * N, XSIDES),
-    (corner_slots, OWN + 4 * N, CORNERS),
+    (range(4), lambda c: [own_slot(j) for j in range(4)], 0, ()),
+    (range(4), y_slots, OWN, (6, 7)),
+    ((2, 3), x_slots, OWN + 2 * N, (4, 0, 1)),
+    ((0, 1), x_slots, OWN + 2 * N, (5, 2, 3)),
 )
 
 
@@ -95,7 +91,7 @@
     forces_ref, energies_ref,
     atoms, xi, basis_0, basis_1, basis_2, basis_3, u_s, a_s, rc_s, ri_s, dens, hid, hid_own, slope,
     msg, gms, tab_t, tab_s, gk, read_t, second, back_t, gm_own, gm_b,
-    gpart, grecv, gsum, fi, fj, fpart, frecv, gs_a, gs_b,
+    gpart, grecv, gsum, fi, fj, fpart, frecv, gs_a, gs_b, poly_s, slant_s,
     pos_ref, valid_ref, spec_ref, table_ref, gain_ref, readout_ref, load_sem,
     send_sem, recv_sem,
 ):
@@ -112,49 +108,65 @@
         load.start()
     own_slots = [own_slot(c) for c in range(4)]
 
+    def turn(g):
+        return jnp.where((g + 4) % 4 >= 2, -1, 1)
+
+    side = turn(gx)
+    own_row = {1: jnp.where(side > 0, 0, 1), 2: jnp.where(side > 0, 1, 0)}
+
+    def peer(dx, dy):
+        return (gx + side * dx, gy + dy)
+
     def there(dx, dy):
         ok = None
-        for d, g, n in ((dx, gx, nx), (dy, gy, ny)):
+        for d, g, n in zip((dx, dy), peer(dx, dy), (nx, ny)):
             if d:
-                one = (g < n - 1) if d > 0 else (g > 0)
+                one = jnp.logical_and(g >= 0, g < n)
                 ok = one if ok is None else jnp.logical_and(ok, one)
         return ok
 
-    def copy(r, n, src, dst, peer):
+    def arrival(n):
+        dx, dy = DIRS[n]
+        if dx == 0:
+            return landing(0), n
+        up = jnp.where(side * turn(gx + side * dx) * dx > 0, 1, 0)
+        return 3 - 3 * up, (2 * up + (1 if dy > 0 else 0) if dy else 4 + up)
+
+    def copy(r, n, arrived, src, dst, device):
         return pltpu.make_async_remote_copy(
-            src_ref=src, dst_ref=dst, send_sem=send_sem.at[r, n], recv_sem=recv_sem.at[r, n],
-            device_id=peer, device_id_type=MESH,
+            src_ref=src, dst_ref=dst, send_sem=send_sem.at[r, n], recv_sem=recv_sem.at[r, arrived],
+            device_id=device, device_id_type=MESH,
         )
 
-    def outward(r, buf, wait, dirs=range(8)):
+    def exchange(r, wait, dirs, src_of, dst_of):
         for n in dirs:
             dx, dy = DIRS[n]
-            src = buf.at[border(dx), border(dy)]
-            dst = buf.at[landing(dx), landing(dy)]
             if wait == "recv":
                 @pl.when(there(-dx, -dy))
                 def _():
-                    copy(r, n, src, dst, (gx - dx, gy - dy)).wait_recv()
+                    dst = dst_of(dx, dy, landing(dx), n)
+                    copy(r, n, n, src_of(dx, dy), dst, peer(-dx, -dy)).wait_recv()
             else:
                 @pl.when(there(dx, dy))
                 def _():
-                    c = copy(r, n, src, dst, (gx + dx, gy + dy))
+                    row, arrived = arrival(n)
+                    dst = dst_of(dx, dy, row, arrived)
+                    c = copy(r, n, arrived, src_of(dx, dy), dst, peer(dx, dy))
                     c.start() if wait == "start" else c.wait_send()
 
+    def outward(r, buf, wait, dirs=range(8)):
+        exchange(
+            r, wait, dirs,
+            lambda dx, dy: buf.at[border(dx), border(dy)],
+            lambda dx, dy, row, n: buf.at[row, landing(dy)],
+        )
+
     def inward(r, buf, land, wait, dirs=range(8)):
-        for n in dirs:
-            dx, dy = DIRS[n]
-            src = buf.at[beyond(dx), beyond(dy)]
-            dst = land.at[n, 0] if dx and dy else land.at[n]
-            if wait == "recv":
-                @pl.when(there(-dx, -dy))
-                def _():
-                    copy(r, n, src, dst, (gx - dx, gy - dy)).wait_recv()
-            else:
-                @pl.when(there(dx, dy))
-                def _():
-                    c = copy(r, n, src, dst, (gx + dx, gy + dy))
-                    c.start() if wait == "start" else c.wait_send()
+        exchange(
+            r, wait, dirs,
+            lambda dx, dy: buf.at[beyond(dx), beyond(dy)],
+            lambda dx, dy, row, n: land.at[n, 0] if dx and dy else land.at[n],
+        )
 
     def returned(land, a, b):
         total = None
@@ -176,16 +188,16 @@
     for dx, dy in DIRS:
         @pl.when(there(dx, dy))
         def _():
-            pl.semaphore_signal(barrier, inc=1, device_id=(gx + dx, gy + dy), device_id_type=MESH)
+            pl.semaphore_signal(barrier, inc=1, device_id=peer(dx, dy), device_id_type=MESH)
     span_x = 1 + jnp.where(gx > 0, 1, 0) + jnp.where(gx < nx - 1, 1, 0)
     span_y = 1 + jnp.where(gy > 0, 1, 0) + jnp.where(gy < ny - 1, 1, 0)
 
     for load in loads:
         load.wait()
     for a, b in own_slots:
-        rows = [pos_ref[i, a - 1, b - 1 : b, :] for i in range(3)]
-        rows.append(valid_ref[a - 1, b - 1 : b, :].astype(F32))
-        rows.append(spec_ref[a - 1, b - 1 : b, :].astype(F32))
+        rows = [pos_ref[i, own_row[a], b - 1 : b, :] for i in range(3)]
+        rows.append(valid_ref[own_row[a], b - 1 : b, :].astype(F32))
+        rows.append(spec_ref[own_row[a], b - 1 : b, :].astype(F32))
         rows.append(jnp.zeros((3, N), F32))
         atoms[a, b] = jnp.concatenate(rows, 0)
 
@@ -242,7 +254,7 @@
                 term = term * u
 
     def part_pairs(c, part):
-        slots_of, lane0, _ = PARTS[part]
+        _, slots_of, lane0, _ = PARTS[part]
         for block in range(BLOCKS):
             for m, (a, b) in enumerate(slots_of(c)):
                 pair_basis(c, block, a, b, lane0 + m * N, part == 0 and m == c)
@@ -265,7 +277,7 @@
         return jnp.concatenate(parts, 1)
 
     def part_density(c, part):
-        slots_of, lane0, _ = PARTS[part]
+        _, slots_of, lane0, _ = PARTS[part]
         slots = slots_of(c)
         out = nt(hot(slots), basis[c][:, lane0 : lane0 + len(slots) * N])
         a, b = own_slots[c]
@@ -275,19 +287,22 @@
             dens[a, b, rows, :] = dens[a, b, rows, :] + piece if part else piece
 
     last = None
-    for part in range(4):
-        if part:
-            outward(0, atoms, "recv", PARTS[part][2])
-        slots_of = PARTS[part][0]
-        for a, b in sorted({slot for c in range(4) for slot in slots_of(c)}):
-            selector(a, b)
-        for c in range(4):
+    for part, (cells, slots_of, _, dirs) in enumerate(PARTS):
+        outward(0, atoms, "recv", dirs)
+        for c in cells:
             part_pairs(c, part)
             if last:
                 part_density(*last)
             last = (c, part)
+        if part == 2:
+            part_density(*last)
+            last = None
+            outward(1, dens, "start", (5, 2, 3))
     part_density(*last)
-    outward(1, dens, "start")
+    outward(1, dens, "start", (0, 1, 4, 6, 7))
+    for a in range(4):
+        for b in range(4):
+            selector(a, b)
 
     def features(slots):
         parts = []
@@ -317,25 +332,25 @@
         return total
 
     def part_message(c, part):
-        slots_of, lane0, _ = PARTS[part]
+        _, slots_of, lane0, _ = PARTS[part]
         slots = slots_of(c)
         h = jnp.concatenate([hid[a, b, :, 0:CH] for a, b in slots], 0)
         return gained(nn(basis[c][:, lane0 : lane0 + len(slots) * N], h))
 
     for c in range(4):
         msg[c] = part_message(c, 0) + hid_own[c]
-    for part in (1, 2):
-        outward(1, dens, "recv", PARTS[part][2])
-        features(sorted({slot for c in range(4) for slot in PARTS[part][0](c)}))
-        for c in range(4):
-            msg[c] += part_message(c, part)
-    outward(1, dens, "recv", CORNERS)
-    features([corner_slots(c)[0] for c in range(4)])
-    for c in range(4):
-        p = msg[c] + part_message(c, 3)
-        s = sigmoid(p)
-        second[c * N : (c + 1) * N, :] = (p * s).astype(BF16)
-        msg[c] = s * (1.0 + p * (1.0 - s))
+    for part in (1, 2, 3):
+        cells, slots_of, _, dirs = PARTS[part]
+        outward(1, dens, "recv", dirs)
+        features(sorted({slot for c in cells for slot in slots_of(c)}))
+        for c in cells:
+            p = msg[c] + part_message(c, part)
+            if part == 1:
+                msg[c] = p
+                continue
+            s = sigmoid(p)
+            second[c * N : (c + 1) * N, :] = (p * s).astype(BF16)
+            msg[c] = s * (1.0 + p * (1.0 - s))
 
     heads = nt(read_t[0:HEADS, :], second[...])
     sh = sigmoid(heads)
@@ -345,7 +360,7 @@
     for c, (a, b) in enumerate(own_slots):
         cols = slice(c * N, (c + 1) * N)
         for h in range(HEADS):
-            energies_ref[h, a - 1, b - 1 : b, :] = out[h : h + 1, cols]
+            energies_ref[h, own_row[a], b - 1 : b, :] = out[h : h + 1, cols]
         tile = jnp.concatenate([back[:, cols], jnp.zeros((N - HEADS, N), F32)], 0)
         back_t[c] = tile.T.astype(BF16)
 
@@ -371,15 +386,54 @@
 
     gpart[...] = jnp.zeros_like(gpart)
     head_grad(0)
-    for c in range(4):
+    for c, complete in GRAD_ORDER:
         if c < 3:
             head_grad(c + 1)
         halo_grad(c)
-        inward(2, gpart, grecv, "start", COMPLETE[c])
-
-    for c, (a, b) in enumerate(own_slots):
+        inward(2, gpart, grecv, "start", complete)
+
+    def own_grad(c):
+        a, b = own_slots[c]
         x = gained(nn(basis[c][:, 0:OWN], gm_b[...])) + gm_own[c]
         gsum[c] = project((x * slope[a, b]).astype(BF16))
+
+    upper, lower, both = slice(0, CH), slice(CH, CH + N), slice(0, CH + N)
+
+    def gradients(c, slots, lanes, buf):
+        h = jnp.concatenate([hid[a, b, :, lanes] for a, b in slots], 0)
+        buf[:, 0 : h.shape[0]] = nt(gms[c, :, lanes], h)
+
+    def horner(c, block, m, lane0, buf):
+        rows = slice(block * ROWS, (block + 1) * ROWS)
+        u = u_s[c, rows, lane0 + m * N : lane0 + (m + 1) * N]
+
+        def grad(k):
+            return buf[k * N + block * ROWS : k * N + (block + 1) * ROWS, m * N : (m + 1) * N]
+
+        poly = grad(RADIAL - 1)
+        slant = poly
+        for k in range(RADIAL - 2, -1, -1):
+            poly = poly * u + grad(k)
+            if k:
+                slant = slant * u + poly
+        return poly, slant * u
+
+    def second_layer_sums(c, buf):
+        for block in range(BLOCKS):
+            rows = slice(block * ROWS, (block + 1) * ROWS)
+            for m in range(5):
+                cols = slice(m * N, (m + 1) * N)
+                poly_s[c, rows, cols], slant_s[c, rows, cols] = horner(c, block, m, OWN, buf)
+
+    gradients(0, halo_slots(0), upper, gs_a)
+    own_grad(0)
+    second_layer_sums(0, gs_a)
+    gradients(1, halo_slots(1), upper, gs_b)
+    own_grad(1)
+    second_layer_sums(1, gs_b)
+    own_grad(2)
+    own_grad(3)
+
     def density_grad(c):
         inward(2, gpart, grecv, "recv", NEEDED[c])
         a, b = own_slot(c)
@@ -398,29 +452,16 @@
 
     fj[...] = jnp.zeros_like(fj)
 
-    def gradients(step, buf):
-        c = step % 4
-        slots = halo_slots(c) if step < 4 else own_slots
-        h = jnp.concatenate([hid[a, b] for a, b in slots], 0)
-        buf[:, 0 : h.shape[0]] = nt(gms[c], h)
-
     def block_forces(c, block, slots, lane0, buf):
         rows = slice(block * ROWS, (block + 1) * ROWS)
         sums = [jnp.zeros((ROWS, N), F32) for _ in range(3)]
         for m, (a, b) in enumerate(slots):
             cols = slice(lane0 + m * N, lane0 + (m + 1) * N)
-            u = u_s[c, rows, cols]
-
-            def grad(k):
-                return buf[k * N + block * ROWS : k * N + (block + 1) * ROWS, m * N : (m + 1) * N]
-
-            poly = grad(RADIAL - 1)
-            slant = poly
-            for k in range(RADIAL - 2, -1, -1):
-                poly = poly * u + grad(k)
-                if k:
-                    slant = slant * u + poly
-            slant = slant * u
+            poly, slant = horner(c, block, m, lane0, buf)
+            if lane0 and c < 2:
+                halo = slice(m * N, (m + 1) * N)
+                poly = poly + poly_s[c, rows, halo]
+                slant = slant + slant_s[c, rows, halo]
             reach = rc_s[c, rows, cols]
             inner = ri_s[c, rows, cols] * slant * (2.0 / SPACE) - poly * (2.0 / SPACE**2)
             force = a_s[c, rows, cols] * (reach * inner - poly * (4.0 / CUT**2))
@@ -437,11 +478,13 @@
             else:
                 fi[c, i, rows, :] += sums[i]
 
-    def pair_forces(step, buf):
-        c = step % 4
-        slots, lane0 = (halo_slots(c), OWN) if step < 4 else (own_slots, 0)
+    def halo_forces(c, buf):
         for block in range(BLOCKS):
-            block_forces(c, block, slots, lane0, buf)
+            block_forces(c, block, halo_slots(c), OWN, buf)
+
+    def own_forces(c, buf):
+        for block in range(BLOCKS):
+            block_forces(c, block, own_slots, 0, buf)
 
     def halo_force(n):
         dx, dy = DIRS[n]
@@ -450,21 +493,35 @@
                 rows = [jnp.sum(fj[a, b, i], 0, keepdims=True) for i in range(3)]
                 fpart[a, b] = jnp.concatenate(rows + [jnp.zeros((5, N), F32)], 0)
 
-    bufs = (gs_a, gs_b)
+    def send_forces(dirs):
+        for n in dirs:
+            halo_force(n)
+        inward(3, fpart, frecv, "start", dirs)
+
+    density_grad(2)
+    gradients(2, halo_slots(2), both, gs_a)
+    density_grad(3)
+    halo_forces(2, gs_a)
+    gradients(3, halo_slots(3), both, gs_b)
+    send_forces((2,))
+    halo_forces(3, gs_b)
+    send_forces((3, 5))
     density_grad(0)
-    gradients(0, gs_a)
-    for step in range(4):
-        if step < 3:
-            density_grad(step + 1)
-        pair_forces(step, bufs[step % 2])
-        gradients(step + 1, bufs[(step + 1) % 2])
-        for n in COMPLETE[step]:
-            halo_force(n)
-        inward(3, fpart, frecv, "start", COMPLETE[step])
-    for step in range(4, 8):
-        pair_forces(step, bufs[step % 2])
-        if step < 7:
-            gradients(step + 1, bufs[(step + 1) % 2])
+    gradients(0, halo_slots(0), lower, gs_a)
+    density_grad(1)
+    halo_forces(0, gs_a)
+    gradients(1, halo_slots(1), lower, gs_b)
+    send_forces((0, 6))
+    halo_forces(1, gs_b)
+    gradients(0, own_slots, both, gs_a)
+    send_forces((1, 4, 7))
+    own_forces(0, gs_a)
+    gradients(1, own_slots, both, gs_b)
+    own_forces(1, gs_b)
+    gradients(2, own_slots, both, gs_a)
+    own_forces(2, gs_a)
+    gradients(3, own_slots, both, gs_b)
+    own_forces(3, gs_b)
     sums = []
     for c in range(4):
         a, b = own_slot(c)
@@ -473,21 +530,16 @@
             mine = jnp.sum(fi[c, i].T, 0, keepdims=True)
             rows.append(jnp.sum(fj[a, b, i], 0, keepdims=True) - mine)
         sums.append(jnp.concatenate(rows + [jnp.zeros((5, N), F32)], 0))
+    outward(0, atoms, "send")
+    outward(1, dens, "send")
+    inward(2, gpart, grecv, "send")
+    inward(3, fpart, frecv, "send")
     inward(3, fpart, frecv, "recv")
     for c in range(4):
         a, b = own_slot(c)
         total = sums[c] + returned(frecv, a, b)
         for i in range(3):
-            forces_ref[i, a - 1, b - 1 : b, :] = total[i : i + 1]
-    outward(0, atoms, "send")
-    outward(1, dens, "send")
-    inward(2, gpart, grecv, "send")
-    inward(3, fpart, frecv, "send")
-
-
-def hand_over(forces_ref, energies_ref, forces_out, energies_out):
-    forces_out[...] = forces_ref[...]
-    energies_out[...] = energies_ref[...]
+            forces_ref[i, own_row[a], b - 1 : b, :] = total[i : i + 1]
 
 
 def shards(nx, ny, positions, valid_mask, species, density_table, radial_gain, readout):
@@ -536,6 +588,8 @@
             vmem((8, 2, 8, N), F32),
             vmem((RADIAL * N, HALO), F32),
             vmem((RADIAL * N, HALO), F32),
+            vmem((2, N, HALO), F32),
+            vmem((2, N, HALO), F32),
             vmem((3, 2, 2, N), F32),
             vmem((2, 2, N), jnp.int32),
             vmem((2, 2, N), jnp.int32),

time: 41.8 us -> 41.2 us (0.986)
  the two profiles are of different devices: /device:TPU:160 before, /device:TPU:95 now
where the time goes in v4:
time: 41.2 us; the launch traced here: 40.6 us
  Pallas kernels  38.7 us (94%)
  local copies, waits for them, and re-layouts  1.21 us (3%)
  between operations  0.64 us (2%)
    pallas_call x1, Pallas kernels, shards(): pl.pallas_call(functools.partial(kernel, nx, ny), out_shape=(pltpu.VMEM((...  38.7 us
    unnamed x2, local copies, waits for them, and re-layouts  1.21 us

profile of v4, /device:TPU:95, one launch (start us, length us, event | category | flops | bytes accessed | tf_op | source)
XLA Modules:
  0.0 40.6 jit_solution(9128174193443925669)
XLA Ops:
  0.6 38.7 %shard_map.77 = (f32[3,2,2,128]{3,2,1,0:T(2,128)S(1)}, f32[16,2,2,128]{3,2,1,0:T(2,128)S(1)}) custom-call(f32[3,2,2,128]{3,2,1,0:T(2,128)} %pos_hbm.1, s32[2,2,128]{2,1,0:T(2,128)} %valid_hbm.1, s32[2,2,128]{2,1,0:T(2,128)} %spec_hbm.1, f32[32,256]{1,0:T(8,128)} %table_hbm.1, f32[8,256]{1,0:T(8,128)} %gain_hbm.1, bf16[16,256]{1,0:T(8,128)(2,1)} %bitcast.1), custom_call_target="tpu_custom_call" | custom-call | tf_op jit(solution)/shard_map/pallas_call | solution.py:549
  39.4 0.6 %copy.10 = f32[3,2,2,128]{3,2,1,0:T(2,128)} copy(f32[3,2,2,128]{3,2,1,0:T(2,128)S(1)} %get-tuple-element.2) | data formatting | bytes 12288
  40.0 0.6 %copy.11 = f32[16,2,2,128]{3,2,1,0:T(2,128)} copy(f32[16,2,2,128]{3,2,1,0:T(2,128)S(1)} %get-tuple-element.3) | data formatting | bytes 65536

commit v5 on v4

--- a/solution.py
+++ b/solution.py
@@ -77,7 +77,8 @@
     (range(4), lambda c: [own_slot(j) for j in range(4)], 0, ()),
     (range(4), y_slots, OWN, (6, 7)),
     ((2, 3), x_slots, OWN + 2 * N, (4, 0, 1)),
-    ((0, 1), x_slots, OWN + 2 * N, (5, 2, 3)),
+    ((0, 1), lambda c: x_slots(c)[:2], OWN + 2 * N, (5,)),
+    ((0, 1), lambda c: x_slots(c)[2:], OWN + 4 * N, (2, 3)),
 )
 
 
@@ -339,13 +340,13 @@
 
     for c in range(4):
         msg[c] = part_message(c, 0) + hid_own[c]
-    for part in (1, 2, 3):
+    for part in (1, 2, 3, 4):
         cells, slots_of, _, dirs = PARTS[part]
         outward(1, dens, "recv", dirs)
         features(sorted({slot for c in cells for slot in slots_of(c)}))
         for c in cells:
             p = msg[c] + part_message(c, part)
-            if part == 1:
+            if part in (1, 3):
                 msg[c] = p
                 continue
             s = sigmoid(p)

time: 41.2 us -> 41.2 us (level)
  no operation moved by 1% of the time
where the time goes in v5:
time: 41.2 us; the launch traced here: 40.7 us
  Pallas kernels  38.8 us (94%)
  local copies, waits for them, and re-layouts  1.21 us (3%)
  between operations  0.64 us (2%)
    pallas_call x1, Pallas kernels, shards(): pl.pallas_call(functools.partial(kernel, nx, ny), out_shape=(pltpu.VMEM((...  38.8 us
    unnamed x2, local copies, waits for them, and re-layouts  1.21 us

profile of v5, /device:TPU:95, one launch (start us, length us, event | category | flops | bytes accessed | tf_op | source)
XLA Modules:
  0.0 40.7 jit_solution(8602380006732263066)
XLA Ops:
  0.6 38.8 %shard_map.77 = (f32[3,2,2,128]{3,2,1,0:T(2,128)S(1)}, f32[16,2,2,128]{3,2,1,0:T(2,128)S(1)}) custom-call(f32[3,2,2,128]{3,2,1,0:T(2,128)} %pos_hbm.1, s32[2,2,128]{2,1,0:T(2,128)} %valid_hbm.1, s32[2,2,128]{2,1,0:T(2,128)} %spec_hbm.1, f32[32,256]{1,0:T(8,128)} %table_hbm.1, f32[8,256]{1,0:T(8,128)} %gain_hbm.1, bf16[16,256]{1,0:T(8,128)(2,1)} %bitcast.1), custom_call_target="tpu_custom_call" | custom-call | tf_op jit(solution)/shard_map/pallas_call | solution.py:550
  39.5 0.6 %copy.10 = f32[3,2,2,128]{3,2,1,0:T(2,128)} copy(f32[3,2,2,128]{3,2,1,0:T(2,128)S(1)} %get-tuple-element.2) | data formatting | bytes 12288
  40.1 0.6 %copy.11 = f32[16,2,2,128]{3,2,1,0:T(2,128)} copy(f32[16,2,2,128]{3,2,1,0:T(2,128)S(1)} %get-tuple-element.3) | data formatting | bytes 65536
